TPU v7x, 32 devices: a whole 2x2x4 slice. The times are simulated.
32 devices in a mesh: dp: 16 (over z, y, x), tensor: 2 (over core).
Axes of the slice: x: 2, y: 2, z: 4, core: 2. Of those that a mesh axis runs over, the one named last changes fastest.
Arguments:
- hidden_in: bfloat16 [32768, 768], P(('dp', 'tensor')), may hold values from -6 to 6
- out_grad: bfloat16 [32768, 768], P(('dp', 'tensor')), may hold values from -6 to 6
- seq_lengths: int32 [16, 8], P('dp'), may hold values from 1 to 1024, as said below
- attn_gain: bfloat16 [768], P('dp'), may hold values from 0.099609375 to 1.8984375
- attn_shift: bfloat16 [768], P('dp'), may hold values from -1.75 to 1.75
- mlp_gain: bfloat16 [768], P('dp'), may hold values from 0.099609375 to 1.8984375
- mlp_shift: bfloat16 [768], P('dp'), may hold values from -1.75 to 1.75
- qkv_weight: bfloat16 [768, 12, 192], P('dp', 'tensor'), may hold values from -0.21875 to 0.21875
- qkv_bias: bfloat16 [2304], P('dp'), may hold values from -1.75 to 1.75
- dense_weight: bfloat16 [768, 12, 64], P('dp', 'tensor'), may hold values from -0.875 to 0.875
- dense_bias: bfloat16 [768], P('dp'), may hold values from -1.75 to 1.75
- fc_weight: bfloat16 [768, 3072], P('dp', 'tensor'), may hold values from -0.21875 to 0.21875
- fc_bias: bfloat16 [3072], P('dp'), may hold values from -1.75 to 1.75
- proj_weight: bfloat16 [768, 3072], P('dp', 'tensor'), may hold values from -0.15625 to 0.15625
- proj_bias: bfloat16 [768], P('dp'), may hold values from -1.75 to 1.75
Outputs:
- block_out: bfloat16 [32768, 768], P(('dp', 'tensor'))
- input_grad: float32 [32768, 768], P(('dp', 'tensor'))
- attn_gain_grad: float32 [768], P(('dp', 'tensor'))
- attn_shift_grad: float32 [768], P(('dp', 'tensor'))
- mlp_gain_grad: float32 [768], P(('dp', 'tensor'))
- mlp_shift_grad: float32 [768], P(('dp', 'tensor'))
- qkv_weight_grad: float32 [768, 12, 192], P('dp', 'tensor')
- qkv_bias_grad: float32 [2304], P(('dp', 'tensor'))
- dense_weight_grad: float32 [768, 12, 64], P('dp', 'tensor')
- dense_bias_grad: float32 [768], P(('dp', 'tensor'))
- fc_weight_grad: float32 [768, 3072], P('dp', 'tensor')
- fc_bias_grad: float32 [3072], P(('dp', 'tensor'))
- proj_weight_grad: float32 [768, 3072], P('dp', 'tensor')
- proj_bias_grad: float32 [768], P(('dp', 'tensor'))
Inputs may be any that keep to these rules, and one draw needn't show every extreme that they name: `seq_lengths`: row g lists the 8 sequences of group g in order; they are all 1 or longer and sum to 2048. One sequence of each row has exactly 1024 rows and covers rows 1023 and 1024 of its group.
All inputs are finite; a program needn't handle non-finite values.
Results may differ from a plain program's by a relative error of at most 0.012.
Values may be sent and summed in bfloat16 or wider, within the bound.
A program may use at most 256 MiB of HBM per device.

v0:
```python
import jax
import jax.numpy as jnp
from jax import lax
from jax.sharding import PartitionSpec as P


def layout(lengths, group_rows):
    seq_ends = jnp.cumsum(lengths)
    starts = seq_ends - lengths
    row_index = jnp.arange(group_rows, dtype=jnp.int32)
    seg_ids = jnp.sum((row_index[:, None] >= seq_ends[None, :]).astype(jnp.int32), axis=1)
    owner_mask = seg_ids[:, None] == jnp.arange(lengths.shape[0], dtype=jnp.int32)[None, :]
    positions = row_index - jnp.sum(jnp.where(owner_mask, starts[None, :], 0), axis=1)
    return (seg_ids, positions)


def layer_norm(values, gain_vec, shift_vec):
    average = jnp.mean(values, axis=-1, keepdims=True)
    centred = values - average
    spread = jnp.mean(centred * centred, axis=-1, keepdims=True)
    return centred * lax.rsqrt(spread + 1e-05) * gain_vec + shift_vec


def rotary_tables(positions, head_dim):
    rot_dims = head_dim // 4
    half_rot = rot_dims // 2
    inv_freq = 10000.0 ** (-(jnp.arange(half_rot, dtype=jnp.float32) * 2.0 / rot_dims))
    angles = positions.astype(jnp.float32)[:, None] * inv_freq[None, :]
    angles = jnp.concatenate([angles, angles], axis=-1)
    return (jnp.cos(angles), jnp.sin(angles))


def rotate(vectors, cosine_table, sine_table):
    rot_dims = cosine_table.shape[-1]
    half_rot = rot_dims // 2
    rot_part = vectors[..., :rot_dims]
    turned = jnp.concatenate([-rot_part[..., half_rot:], rot_part[..., :half_rot]], axis=-1)
    result = rot_part * cosine_table[:, None, :] + turned * sine_table[:, None, :]
    return jnp.concatenate([result, vectors[..., rot_dims:]], axis=-1)


def exact_gelu(values):
    return jax.nn.gelu(values, approximate=False)


def body(
    hidden_in,
    out_grad,
    seq_lengths,
    attn_gain,
    attn_shift,
    mlp_gain,
    mlp_shift,
    qkv_weight,
    qkv_bias,
    dense_weight,
    dense_bias,
    fc_weight,
    fc_bias,
    proj_weight,
    proj_bias,
):
    tensor_index = lax.axis_index("tensor")
    tensor_count = lax.axis_size("tensor")
    local_rows = hidden_in.shape[0]
    group_rows = local_rows * tensor_count
    gathered = (
        lax.all_gather(qkv_weight, "dp", axis=0, tiled=True),
        lax.all_gather(dense_weight, "dp", axis=0, tiled=True),
        lax.all_gather(fc_weight, "dp", axis=0, tiled=True),
        lax.all_gather(proj_weight, "dp", axis=0, tiled=True),
        lax.all_gather(attn_gain, "dp", axis=0, tiled=True),
        lax.all_gather(attn_shift, "dp", axis=0, tiled=True),
        lax.all_gather(mlp_gain, "dp", axis=0, tiled=True),
        lax.all_gather(mlp_shift, "dp", axis=0, tiled=True),
        lax.all_gather(qkv_bias, "dp", axis=0, tiled=True),
        lax.all_gather(dense_bias, "dp", axis=0, tiled=True),
        lax.all_gather(fc_bias, "dp", axis=0, tiled=True),
        lax.all_gather(proj_bias, "dp", axis=0, tiled=True),
    )
    (
        w_qkv,
        w_dense,
        w_fc,
        w_proj,
        gain_attn,
        shift_attn,
        gain_mlp,
        shift_mlp,
        bias_qkv,
        bias_dense,
        bias_fc,
        bias_proj,
    ) = gathered
    model_width = w_qkv.shape[0]
    head_count = w_qkv.shape[1]
    triple_width = w_qkv.shape[2]
    head_dim = w_dense.shape[2]
    hidden_units = w_fc.shape[1]
    qkv_cols = head_count * triple_width
    attn_cols = head_count * head_dim
    my_bias_qkv = lax.dynamic_slice_in_dim(bias_qkv, tensor_index * qkv_cols, qkv_cols).astype(
        jnp.float32
    )
    my_bias_fc = lax.dynamic_slice_in_dim(
        bias_fc, tensor_index * hidden_units, hidden_units
    ).astype(jnp.float32)
    gain_attn_f = gain_attn.astype(jnp.float32)
    shift_attn_f = shift_attn.astype(jnp.float32)
    gain_mlp_f = gain_mlp.astype(jnp.float32)
    shift_mlp_f = shift_mlp.astype(jnp.float32)
    seg_ids, positions = layout(seq_lengths[0], group_rows)
    x_rows = hidden_in.astype(jnp.float32)

    def norms(values, gain_one, shift_one, gain_two, shift_two):
        return (layer_norm(values, gain_one, shift_one), layer_norm(values, gain_two, shift_two))

    (normed_one, normed_two), norm_back = jax.vjp(
        norms, x_rows, gain_attn_f, shift_attn_f, gain_mlp_f, shift_mlp_f
    )
    normed_attn, normed_mlp = (
        lax.all_gather(normed_one.astype(jnp.bfloat16), "tensor", axis=0, tiled=True),
        lax.all_gather(normed_two.astype(jnp.bfloat16), "tensor", axis=0, tiled=True),
    )
    merged_lin = (
        jnp.dot(
            normed_attn, w_qkv.reshape(model_width, qkv_cols), preferred_element_type=jnp.float32
        )
        + my_bias_qkv
    )
    merged_lin = merged_lin.reshape(group_rows, head_count, triple_width)
    cosine_table, sine_table = rotary_tables(positions, head_dim)

    def turn_pair(query_lin, key_lin):
        return (
            rotate(query_lin, cosine_table, sine_table),
            rotate(key_lin, cosine_table, sine_table),
        )

    (query_rot, key_rot), turn_back = jax.vjp(
        turn_pair, merged_lin[..., :head_dim], merged_lin[..., head_dim : 2 * head_dim]
    )
    query_low = query_rot.astype(jnp.bfloat16)
    key_low = key_rot.astype(jnp.bfloat16)
    value_low = merged_lin[..., 2 * head_dim :].astype(jnp.bfloat16)
    score_scale = head_dim ** (-0.5)
    block_rows = min(512, group_rows)
    block_count = group_rows // block_rows
    row_index = jnp.arange(group_rows, dtype=jnp.int32)

    def masked_scores(number):
        begin_row = number * block_rows
        end_row = begin_row + block_rows
        scores = (
            jnp.einsum(
                "qhd,khd->hqk",
                query_low[begin_row:end_row],
                key_low[:end_row],
                preferred_element_type=jnp.float32,
            )
            * score_scale
        )
        allowed = (row_index[None, :end_row] <= row_index[begin_row:end_row, None]) & (
            seg_ids[None, :end_row] == seg_ids[begin_row:end_row, None]
        )
        return jnp.where(allowed[None], scores, -1e30)

    head_blocks = []
    log_totals = []
    for number in range(block_count):
        end_row = (number + 1) * block_rows
        scores = masked_scores(number)
        peak_score = jnp.max(scores, axis=-1, keepdims=True)
        weights = jnp.exp(scores - peak_score)
        norm_total = jnp.sum(weights, axis=-1, keepdims=True)
        log_totals.append(peak_score + jnp.log(norm_total))
        prob_low = (weights / norm_total).astype(jnp.bfloat16)
        head_blocks.append(
            jnp.einsum(
                "hqk,khd->qhd", prob_low, value_low[:end_row], preferred_element_type=jnp.float32
            )
        )
    heads_flat = (
        jnp.concatenate(head_blocks, axis=0).astype(jnp.bfloat16).reshape(group_rows, attn_cols)
    )
    attn_part = jnp.einsum(
        "gc,dc->gd",
        heads_flat,
        w_dense.reshape(model_width, attn_cols),
        preferred_element_type=jnp.float32,
    )
    fc_pre = jnp.dot(normed_mlp, w_fc, preferred_element_type=jnp.float32) + my_bias_fc
    act_full, gelu_back = jax.vjp(exact_gelu, fc_pre)
    act_low = act_full.astype(jnp.bfloat16)
    mlp_part = jnp.einsum("gf,df->gd", act_low, w_proj, preferred_element_type=jnp.float32)
    branch_rows = lax.psum_scatter(
        (attn_part + mlp_part).astype(jnp.bfloat16), "tensor", scatter_dimension=0, tiled=True
    ).astype(jnp.float32)
    block_out = (
        x_rows + branch_rows + bias_dense.astype(jnp.float32) + bias_proj.astype(jnp.float32)
    ).astype(jnp.bfloat16)
    w_qkv, w_dense, w_fc, w_proj = (
        lax.all_gather(qkv_weight, "dp", axis=0, tiled=True),
        lax.all_gather(dense_weight, "dp", axis=0, tiled=True),
        lax.all_gather(fc_weight, "dp", axis=0, tiled=True),
        lax.all_gather(proj_weight, "dp", axis=0, tiled=True),
    )
    cot_all = lax.all_gather(out_grad, "tensor", axis=0, tiled=True)
    grad_act = jnp.dot(cot_all, w_proj, preferred_element_type=jnp.float32)
    grad_proj = jnp.einsum("gd,gf->df", cot_all, act_low, preferred_element_type=jnp.float32)
    grad_pre = gelu_back(grad_act)[0].astype(jnp.bfloat16)
    grad_fc = jnp.einsum("gd,gf->df", normed_mlp, grad_pre, preferred_element_type=jnp.float32)
    fc_bias_part = jnp.sum(grad_pre, axis=0, dtype=jnp.float32)
    grad_normed_mlp = jnp.einsum("gf,df->gd", grad_pre, w_fc, preferred_element_type=jnp.float32)
    dense_flat = w_dense.reshape(model_width, attn_cols)
    grad_heads = (
        jnp.dot(cot_all, dense_flat, preferred_element_type=jnp.float32)
        .astype(jnp.bfloat16)
        .reshape(group_rows, head_count, head_dim)
    )
    grad_dense = jnp.einsum(
        "gd,gc->dc", cot_all, heads_flat, preferred_element_type=jnp.float32
    ).reshape(model_width, head_count, head_dim)
    query_grads = []
    grad_key = jnp.zeros((group_rows, head_count, head_dim), jnp.float32)
    grad_value = jnp.zeros((group_rows, head_count, head_dim), jnp.float32)
    for number in range(block_count):
        begin_row = number * block_rows
        end_row = begin_row + block_rows
        probs = jnp.exp(masked_scores(number) - log_totals[number])
        heads_blk = grad_heads[begin_row:end_row]
        grad_probs = jnp.einsum(
            "qhd,khd->hqk", heads_blk, value_low[:end_row], preferred_element_type=jnp.float32
        )
        row_delta = jnp.sum(probs * grad_probs, axis=-1, keepdims=True)
        grad_scores = (probs * (grad_probs - row_delta)).astype(jnp.bfloat16)
        query_grads.append(
            jnp.einsum(
                "hqk,khd->qhd", grad_scores, key_low[:end_row], preferred_element_type=jnp.float32
            )
            * score_scale
        )
        grad_key = grad_key.at[:end_row].add(
            jnp.einsum(
                "hqk,qhd->khd",
                grad_scores,
                query_low[begin_row:end_row],
                preferred_element_type=jnp.float32,
            )
            * score_scale
        )
        grad_value = grad_value.at[:end_row].add(
            jnp.einsum(
                "hqk,qhd->khd",
                probs.astype(jnp.bfloat16),
                heads_blk,
                preferred_element_type=jnp.float32,
            )
        )
    grad_query = jnp.concatenate(query_grads, axis=0)
    grad_query_lin, grad_key_lin = turn_back((grad_query, grad_key))
    grad_merged = (
        jnp.concatenate([grad_query_lin, grad_key_lin, grad_value], axis=-1)
        .astype(jnp.bfloat16)
        .reshape(group_rows, qkv_cols)
    )
    grad_qkv = jnp.einsum(
        "gd,gc->dc", normed_attn, grad_merged, preferred_element_type=jnp.float32
    ).reshape(model_width, head_count, triple_width)
    qkv_bias_part = jnp.sum(grad_merged, axis=0, dtype=jnp.float32)
    grad_normed_attn = jnp.einsum(
        "gc,dc->gd",
        grad_merged,
        w_qkv.reshape(model_width, qkv_cols),
        preferred_element_type=jnp.float32,
    )
    cot_rows = out_grad.astype(jnp.float32)
    local_attn, local_mlp = (
        lax.psum_scatter(
            grad_normed_attn.astype(jnp.bfloat16), "tensor", scatter_dimension=0, tiled=True
        ).astype(jnp.float32),
        lax.psum_scatter(
            grad_normed_mlp.astype(jnp.bfloat16), "tensor", scatter_dimension=0, tiled=True
        ).astype(jnp.float32),
    )
    grad_x, grad_gain_attn, grad_shift_attn, grad_gain_mlp, grad_shift_mlp = norm_back(
        (local_attn, local_mlp)
    )
    input_grad = cot_rows + grad_x
    cot_sums = jnp.sum(cot_rows, axis=0)
    full_qkv_bias = lax.dynamic_update_slice_in_dim(
        jnp.zeros((qkv_cols * tensor_count,), jnp.float32),
        qkv_bias_part,
        tensor_index * qkv_cols,
        0,
    )
    full_fc_bias = lax.dynamic_update_slice_in_dim(
        jnp.zeros((hidden_units * tensor_count,), jnp.float32),
        fc_bias_part,
        tensor_index * hidden_units,
        0,
    )
    small_sums = (
        lax.psum_scatter(grad_gain_attn, ("dp", "tensor"), scatter_dimension=0, tiled=True),
        lax.psum_scatter(grad_shift_attn, ("dp", "tensor"), scatter_dimension=0, tiled=True),
        lax.psum_scatter(grad_gain_mlp, ("dp", "tensor"), scatter_dimension=0, tiled=True),
        lax.psum_scatter(grad_shift_mlp, ("dp", "tensor"), scatter_dimension=0, tiled=True),
        lax.psum_scatter(full_qkv_bias, ("dp", "tensor"), scatter_dimension=0, tiled=True),
        lax.psum_scatter(cot_sums, ("dp", "tensor"), scatter_dimension=0, tiled=True),
        lax.psum_scatter(full_fc_bias, ("dp", "tensor"), scatter_dimension=0, tiled=True),
    )
    large_sums = (
        lax.psum_scatter(grad_qkv, "dp", scatter_dimension=0, tiled=True),
        lax.psum_scatter(grad_dense, "dp", scatter_dimension=0, tiled=True),
        lax.psum_scatter(grad_fc, "dp", scatter_dimension=0, tiled=True),
        lax.psum_scatter(grad_proj, "dp", scatter_dimension=0, tiled=True),
    )
    return (
        block_out,
        input_grad,
        small_sums[0],
        small_sums[1],
        small_sums[2],
        small_sums[3],
        large_sums[0],
        small_sums[4],
        large_sums[1],
        small_sums[5],
        large_sums[2],
        small_sums[6],
        large_sums[3],
        small_sums[5],
    )


def solution(mesh):
    in_specs = (
        P(("dp", "tensor"), None),
        P(("dp", "tensor"), None),
        P("dp", None),
        P("dp"),
        P("dp"),
        P("dp"),
        P("dp"),
        P("dp", "tensor", None),
        P("dp"),
        P("dp", "tensor", None),
        P("dp"),
        P("dp", "tensor"),
        P("dp"),
        P("dp", "tensor"),
        P("dp"),
    )
    out_specs = (
        P(("dp", "tensor"), None),
        P(("dp", "tensor"), None),
        P(("dp", "tensor")),
        P(("dp", "tensor")),
        P(("dp", "tensor")),
        P(("dp", "tensor")),
        P("dp", "tensor", None),
        P(("dp", "tensor")),
        P("dp", "tensor", None),
        P(("dp", "tensor")),
        P("dp", "tensor"),
        P(("dp", "tensor")),
        P("dp", "tensor"),
        P(("dp", "tensor")),
    )
    return jax.shard_map(body, mesh=mesh, in_specs=in_specs, out_specs=out_specs, check_vma=False)
```

profile of v0, /device:TPU:0, one launch (start us, length us, event | category | flops | bytes accessed | tf_op | source)
XLA Modules:
  0.0 1064.3 jit_solution(6079659336549797893)
XLA Ops:
  18.7 79.0 %all-reduce.26 = (bf16[768]{0:T(1024)(128)(2,1)S(1)}, bf16[768]{0:T(1024)(128)(2,1)S(1)}, bf16[3072]{0:T(1024)(128)(2,1)S(1)}, bf16[768]{0:T(1024)(128)(2,1)S(1)...) all-reduce(bf16[768]{0:T(1024)(128)(2,1)S(1)} %dynamic-update-slice, ...), channel_id=1, replica_groups=mesh['dp'=16,'tensor'=2] {'dp'}, use_global_device_ids=true, to_apply=%add.14 | all-reduce | flops 9984 | bytes 39936
  105.9 44.1 %all_gather.54 = bf16[768,6,64]{2,0,1:T(8,128)(2,1)S(1)} all-gather(bf16[48,6,64]{2,0,1:T(8,128)(2,1)S(1)} %copy-done.50), channel_id=1, replica_groups=mesh['dp'=16,'tensor'=2] {'dp'}, dimensions={0}, use_global_device_ids=true | all-gather | bytes 626688 | tf_op jit(solution)/shard_map/all_gather | solution.py:69
  211.7 8.4 fusion.153
  220.1 9.0 fusion.2
  229.1 12.9 %multiply_reduce_fusion.1 = (f32[6,512]{1,0:T(8,128)S(1)}, f32[6,512,1536]{2,1,0:T(8,128)}) fusion(f32[6,512,1536]{2,1,0:T(8,128)} %get-tuple-element.251, f32[6,512]{1,0:T(8,128)S(1)} %log_add_fusion.1, bf16[512,6,64]{0,2,1:T(8,128)(2,1)} %bitcast.138, bf16[2048,6,192]{0,2,1:T(8,128)(2,1)} %copy-done.9), kind=kOutput, calls=%fused_computation.10 | convolution fusion | flops 618132480 | bytes 39346176 | tf_op jit(solution)/shard_map/qhd,khd->hqk/dot_general | solution.py:232
  242.1 13.0 %multiply_convert_fusion.1 = bf16[6,512,1536]{2,1,0:T(8,128)(2,1)S(1)} fusion(f32[6,512,1536]{2,1,0:T(8,128)} %get-tuple-element.257, f32[6,512,1536]{2,1,0:T(8,128)} %get-tuple-element.251, f32[6,512]{1,0:T(8,128)S(1)} %get-tuple-element.256, f32[6,512]{1,0:T(8,128)S(1)} %log_add_fusion.1), kind=kLoop, calls=%fused_computation.9 | loop fusion | flops 18874368 | bytes 47210496 | tf_op jit(solution)/shard_map/convert_element_type | solution.py:236
  260.8 10.7 %fusion.154 = (f32[6,512]{1,0:T(8,128)S(1)}, f32[6,512,2048]{2,1,0:T(8,128)}) fusion(bf16[512,6,64]{0,2,1:T(8,128)(2,1)S(1)} %copy-done.32, bf16[2048,6,16]{0,2,1:T(8,128)(2,1)S(1)} %get-tuple-element.213, bf16[2048,6,48]{0,2,1:T(8,128)(2,1)S(1)} %get-tuple-element.219, pred[512,2048]{1,0:T(8,128)(4,1)S(1)} %copy-done.38), kind=kOutput, calls=%fused_computation.253 | convolution fusion | flops 827323392 | bytes 28192768 | tf_op jit(solution)/shard_map/qhd,khd->hqk/dot_general | solution.py:155
  271.5 10.5 fusion
  282.0 16.2 %multiply_reduce_fusion = (f32[6,512]{1,0:T(8,128)S(1)}, f32[6,512,2048]{2,1,0:T(8,128)}) fusion(f32[6,512,2048]{2,1,0:T(8,128)} %get-tuple-element.253, f32[6,512]{1,0:T(8,128)S(1)} %log_add_fusion, bf16[512,6,64]{0,2,1:T(8,128)(2,1)S(1)} %bitcast.136, bf16[2048,6,192]{0,2,1:T(8,128)(2,1)} %copy-done.9), kind=kOutput, calls=%fused_computation.1 | convolution fusion | flops 824177664 | bytes 52322304 | tf_op jit(solution)/shard_map/qhd,khd->hqk/dot_general | solution.py:232
  298.2 17.0 %multiply_convert_fusion = bf16[6,512,2048]{2,1,0:T(8,128)(2,1)S(1)} fusion(f32[6,512,2048]{2,1,0:T(8,128)} %get-tuple-element.255, f32[6,512,2048]{2,1,0:T(8,128)} %get-tuple-element.253, f32[6,512]{1,0:T(8,128)S(1)} %get-tuple-element.254, f32[6,512]{1,0:T(8,128)S(1)} %log_add_fusion), kind=kLoop, calls=%fused_computation | loop fusion | flops 25165824 | bytes 62939136 | tf_op jit(solution)/shard_map/convert_element_type | solution.py:236
  325.8 8.0 bitcast_add_fusion.2
  355.8 11.6 %bitcast_add_fusion.1 = bf16[2048,6,64]{0,2,1:T(8,128)(2,1)S(1)} fusion(f32[2048,6,64]{0,2,1:T(8,128)} %fusion.68, bf16[512,6,64]{0,2,1:T(8,128)(2,1)S(1)} %bitcast.137, f32[6,512,2048]{2,1,0:T(8,128)} %get-tuple-element.253, f32[6,512]{1,0:T(8,128)S(1)} %log_add_fusion), kind=kOutput, calls=%fused_computation.109 | convolution fusion | flops 819462144 | bytes 30289920 | tf_op jit(solution)/shard_map/hqk,qhd->khd/dot_general | solution.py:253
  382.5 9.3 fusion.105
  392.5 34.9 %multiply_convert_fusion.3 = (bf16[2048,1536]{1,0:T(8,128)(2,1)}, f32[2048,1536]{1,0:T(8,128)}, f32[2048,1536]{1,0:T(8,128)}) fusion(f32[1536]{0:T(1024)S(1)} %copy-done.64, bf16[2048,768]{1,0:T(8,128)(2,1)} %all-gather.11.cloned.1.call-done, bf16[768,1536]{1,0:T(8,128)(2,1)} %all-gather.13.cloned.1.call-done), kind=kOutput, calls=%fused_computation.25 | convolution fusion | flops 5039456256 | bytes 36968448 | tf_op jit(solution)/shard_map/dot_general | solution.py:192
  427.3 17.0 %convert_reduce_fusion = (f32[1536]{0:T(1024)S(1)}, bf16[2048,1536]{1,0:T(8,128)(2,1)S(1)}) fusion(f32[2048,1536]{1,0:T(8,128)} %get-tuple-element.212, bf16[2048,768]{1,0:T(8,128)(2,1)} %all-gather.17.cloned.1.call-done, bf16[768,1536]{1,0:T(8,128)(2,1)} %all-gather.15.cloned.1.call-done, f32[2048,1536]{1,0:T(8,128)} %get-tuple-element.245, ...), kind=kOutput, calls=%fused_computation.19 | convolution fusion | flops 4885314048 | bytes 36974592 | tf_op jit(solution)/shard_map/dot_general | solution.py:209
  466.0 11.1 %fusion.106 = bf16[6,64,512]{2,1,0:T(8,128)(2,1)S(1)} fusion(f32[6,512,2048]{2,1,0:T(8,128)} %get-tuple-element.253, f32[6,512]{1,0:T(8,128)S(1)} %copy-done.60, f32[6,512]{1,0:T(8,128)S(1)} %copy-done.58, bf16[2048,6,192]{0,2,1:T(8,128)(2,1)} %copy-done.9), kind=kOutput, calls=%fused_computation.174 | convolution fusion | flops 824377344 | bytes 27156480 | tf_op jit(solution)/shard_map/hqk,khd->qhd/dot_general | solution.py:179
  494.4 10.0 fusion.33
  504.5 9.8 fusion.156
  514.4 9.7 convolution_bitcast_fusion
  545.5 37.6 %all-reduce.25 = (f32[768]{0:T(1024)S(1)}, f32[768]{0:T(1024)S(1)}, f32[768]{0:T(1024)S(1)}, f32[768]{0:T(1024)S(1)}, f32[2304]{0:T(1024)S(1)}, /*index=5*/f32[768]{0:T(1024)S(1)}, f32[3072]{0:T(1024)S(1)}) all-reduce(f32[768]{0:T(1024)S(1)} %get-tuple-element.187, ...), channel_id=5, replica_groups=mesh['dp'=16,'tensor'=2] {'dp','tensor'}, use_global_device_ids=true, to_apply=%region_25.26.clone | all-reduce | flops 9216 | bytes 73728
  586.7 45.2 %reduce-scatter.18.cloned.1.call-done = f32[48,6,64]{2,0,1:T(8,128)} async-done(((f32[768,6,64]{2,0,1:T(8,128)}), f32[48,6,64]{2,0,1:T(8,128)}) %reduce-scatter.18.cloned.1.call-update) | async-done | bytes 73744 | tf_op jit(solution)/shard_map/reduce_scatter | solution.py:314
  631.9 141.2 %reduce-scatter.16.cloned.1.call-done = f32[48,6,192]{2,0,1:T(8,128)} async-done(((f32[768,6,192]{2,0,1:T(8,128)}), f32[48,6,192]{2,0,1:T(8,128)}) %reduce-scatter.16.cloned.1.call-update) | async-done | bytes 221200 | tf_op jit(solution)/shard_map/reduce_scatter | solution.py:313
  773.2 142.5 %reduce-scatter.20.cloned.1.call-done = f32[48,1536]{1,0:T(8,128)} async-done(((f32[768,1536]{1,0:T(8,128)}), f32[48,1536]{1,0:T(8,128)}) %reduce-scatter.20.cloned.1.call-update) | async-done | bytes 294928 | tf_op jit(solution)/shard_map/reduce_scatter | solution.py:315
  915.7 141.4 %reduce-scatter.22.cloned.1.call-done = f32[48,1536]{1,0:T(8,128)} async-done(((f32[768,1536]{1,0:T(8,128)}), f32[48,1536]{1,0:T(8,128)}) %reduce-scatter.22.cloned.1.call-update) | async-done | bytes 294928
  (322 shorter events, 196.9 us)
Async XLA Ops:
  7.2 92.2 %copy-start.3 = (bf16[1024,768]{1,0:T(8,128)(2,1)S(1)}, bf16[1024,768]{1,0:T(8,128)(2,1)}, u32[]{:S(2)}) copy-start(bf16[1024,768]{1,0:T(8,128)(2,1)} %param.35) | copy-start | bytes 4718596
  7.2 149.9 %all-gather.17.cloned.1.call-start = ((), (), s32[]{:S(2)}) async-start(), calls=%async_computation.13 | async-start | bytes 4718592 | tf_op jit(solution)/shard_map/all_gather | solution.py:208
  7.9 153.8 %all-gather.9.cloned.1.call-start = ((), (), s32[]{:S(2)}) async-start(), calls=%async_computation.8 | async-start | bytes 2506752 | tf_op jit(solution)/shard_map/all_gather | solution.py:68
  8.7 156.3 %all-gather.7.cloned.1.call-start = ((), (), s32[]{:S(2)}) async-start(), calls=%async_computation.7 | async-start | bytes 4718592 | tf_op jit(solution)/shard_map/all_gather | solution.py:122
  103.2 288.6 %all-gather.11.cloned.1.call-start = ((), (), s32[]{:S(2)}) async-start(), calls=%async_computation.9 | async-start | bytes 4718592 | tf_op jit(solution)/shard_map/all_gather | solution.py:123
  103.8 288.1 %all-gather.13.cloned.1.call-start = ((), (), s32[]{:S(2)}) async-start(), calls=%async_computation.10 | async-start | bytes 2506752 | tf_op jit(solution)/shard_map/all_gather | solution.py:70
  104.4 322.9 %all-gather.15.cloned.1.call-start = ((), (), s32[]{:S(2)}) async-start(), calls=%async_computation.11 | async-start | bytes 2506752 | tf_op jit(solution)/shard_map/all_gather | solution.py:71
  105.0 426.6 %reduce-scatter.14.cloned.1.call-start = ((), (), s32[]{:S(2)}) async-start(), calls=%async_computation.15 | async-start | bytes 4718592 | tf_op jit(solution)/shard_map/reduce_scatter | solution.py:279
  105.9 66.1 %copy-start.33 = (f32[2048,16]{0,1:T(8,128)}, f32[2048,16]{0,1:T(8,128)S(1)}, u32[]{:S(2)}) copy-start(f32[2048,16]{0,1:T(8,128)S(1)} %get-tuple-element.237) | copy-start | bytes 393220
  105.9 66.1 %copy-start.35 = (f32[2048,16]{0,1:T(8,128)}, f32[2048,16]{0,1:T(8,128)S(1)}, u32[]{:S(2)}) copy-start(f32[2048,16]{0,1:T(8,128)S(1)} %get-tuple-element.238) | copy-start | bytes 393220
  171.7 22.8 %copy-start.9 = (bf16[2048,6,192]{0,2,1:T(8,128)(2,1)}, bf16[2048,6,192]{0,2,1:T(8,128)(2,1)S(1)}, u32[]{:S(2)}) copy-start(bf16[2048,6,192]{0,2,1:T(8,128)(2,1)S(1)} %convert.33) | copy-start | bytes 14155780
  171.9 88.8 %copy-start.5 = (bf16[2048,6,48]{0,2,1:T(8,128)(2,1)}, bf16[2048,6,48]{0,2,1:T(8,128)(2,1)S(1)}, u32[]{:S(2)}) copy-start(bf16[2048,6,48]{0,2,1:T(8,128)(2,1)S(1)} %get-tuple-element.219) | copy-start | bytes 3538948
  325.8 18.1 %slice-start = ((s8[12582912]{0:T(1024)(128)(4,1)}), s8[4194304]{0:T(1024)(128)(4,1)S(1)}, s32[]{:S(2)}) async-start(s8[12582912]{0:T(1024)(128)(4,1)} %bitcast.129), calls=%async_computation.20 | async-start | bytes 8388608
  325.8 18.1 %slice-start.1 = ((s8[12582912]{0:T(1024)(128)(4,1)}), s8[4194304]{0:T(1024)(128)(4,1)S(1)}, s32[]{:S(2)}) async-start(s8[12582912]{0:T(1024)(128)(4,1)} %bitcast.129), calls=%async_computation.21 | async-start | bytes 8388608
  325.8 23.6 %slice-start.3 = ((s8[18874368]{0:T(1024)(128)(4,1)}), s8[4194304]{0:T(1024)(128)(4,1)S(1)}, s32[]{:S(2)}) async-start(s8[18874368]{0:T(1024)(128)(4,1)} %bitcast.131), calls=%async_computation.23 | async-start | bytes 8388608
  325.8 23.6 %slice-start.4 = ((s8[18874368]{0:T(1024)(128)(4,1)}), s8[4194304]{0:T(1024)(128)(4,1)S(1)}, s32[]{:S(2)}) async-start(s8[18874368]{0:T(1024)(128)(4,1)} %bitcast.131), calls=%async_computation.24 | async-start | bytes 8388608
  391.8 139.8 %reduce-scatter.12.cloned.1.call-start = ((), (), s32[]{:S(2)}) async-start(), calls=%async_computation.14 | async-start | bytes 4718592 | tf_op jit(solution)/shard_map/reduce_scatter | solution.py:282
  427.3 19.6 %copy-start.68 = (bf16[768,1536]{1,0:T(8,128)(2,1)S(1)}, bf16[768,1536]{1,0:T(8,128)(2,1)}, u32[]{:S(2)}) copy-start(bf16[768,1536]{1,0:T(8,128)(2,1)} %all-gather.13.cloned.1.call-done) | copy-start | bytes 7077892
  453.4 85.6 %reduce-scatter.10.cloned.1.call-start = ((), (), s32[]{:S(2)}) async-start(), calls=%async_computation.12 | async-start | bytes 4718592 | tf_op jit(solution)/shard_map/reduce_scatter | solution.py:196
  489.1 142.9 %reduce-scatter.18.cloned.1.call-start = ((), (), s32[]{:S(2)}) async-start(), calls=%async_computation.17 | async-start | bytes 2506752 | tf_op jit(solution)/shard_map/reduce_scatter | solution.py:314
  494.3 278.8 %reduce-scatter.16.cloned.1.call-start = ((), (), s32[]{:S(2)}) async-start(), calls=%async_computation.16 | async-start | bytes 5013504 | tf_op jit(solution)/shard_map/reduce_scatter | solution.py:313
  504.4 411.2 %reduce-scatter.20.cloned.1.call-start = ((), (), s32[]{:S(2)}) async-start(), calls=%async_computation.18 | async-start | bytes 5013504 | tf_op jit(solution)/shard_map/reduce_scatter | solution.py:315
  514.3 542.7 %reduce-scatter.22.cloned.1.call-start = ((), (), s32[]{:S(2)}) async-start(), calls=%async_computation.19 | async-start | bytes 5013504
  583.8 473.7 %copy-start.71 = (f32[24]{0:T(128)}, f32[24]{0:T(128)S(1)}, u32[]{:S(2)}) copy-start(f32[24]{0:T(128)S(1)} %dynamic-slice.72) | copy-start | bytes 292
  (72 other events, 337.2 us)
Sparse Core Ops, SparseCore 0:
  9.6 14.8 all-gather.16
  27.1 64.0 all-gather.8
  103.4 7.9 all-gather.6
  112.8 13.2 all-gather.10
  128.8 63.9 all-gather.12
  195.5 61.1 all-gather.14
  391.9 8.4 reduce-scatter.13
  453.5 8.4 reduce-scatter.11
  489.2 7.8 reduce-scatter.9
  503.2 128.6 reduce-scatter.17
  637.7 135.4 reduce-scatter.15
  779.6 136.0 reduce-scatter.19
  921.4 135.5 reduce-scatter.21
where the time goes:
time: 1070 us; the launch traced here: 1060 us
  waiting for transfers between devices  473 us (44%)
  matrix products  264 us (25%)
  blocking collectives  161 us (15%)
  other arithmetic  102 us (10%)
  local copies, waits for them, and re-layouts  46.6 us (4%)
  between operations  17.3 us (2%)
    unnamed x14, waiting for transfers between devices  144 us
    reduce_scatter x1, waiting for transfers between devices, body(): lax.psum_scatter(grad_fc, 'dp', scatter_dimension=0, tiled=True)  142 us
    reduce_scatter x1, waiting for transfers between devices, body(): lax.psum_scatter(grad_qkv, 'dp', scatter_dimension=0, tiled=True)  141 us
    unnamed x2, blocking collectives  117 us
    reduce_scatter x1, waiting for transfers between devices, body(): lax.psum_scatter(grad_dense, 'dp', scatter_dimension=0, tiled=True)  45.2 us
    all_gather x1, blocking collectives, body(): lax.all_gather(dense_weight, 'dp', axis=0, tiled=True)  44.1 us
    convert_element_type x4, other arithmetic, body(): grad_scores = (probs * (grad_probs - row_delta)).astype(jnp.bfloat16)  40.9 us
    dot_general x4, matrix products, body(): jnp.einsum('qhd,khd->hqk', heads_blk, value_low[:end_row], preferred_elem...  39.2 us
  transfers between devices with their start and end apart: 13, of which 4 were waited for; matrix products, arithmetic and copies ran while one was open for 37% of the time, Pallas kernels for 0%

commit v1 on v0

--- a/solution.py
+++ b/solution.py
@@ -5,7 +5,10 @@
 
 
 def layout(lengths, group_rows):
-    seq_ends = jnp.cumsum(lengths)
+    seq_index = jnp.arange(lengths.shape[0], dtype=jnp.int32)
+    seq_ends = jnp.sum(
+        jnp.where(seq_index[None, :] <= seq_index[:, None], lengths[None, :], 0), axis=1
+    )
     starts = seq_ends - lengths
     row_index = jnp.arange(group_rows, dtype=jnp.int32)
     seg_ids = jnp.sum((row_index[:, None] >= seq_ends[None, :]).astype(jnp.int32), axis=1)

time: 1070 us -> 1070 us (level)
  no operation moved by 1% of the time
where the time goes in v1:
time: 1070 us
  waiting for transfers between devices  475 us (44%)
  matrix products  264 us (25%)
  blocking collectives  161 us (15%)
  other arithmetic  101 us (9%)
  local copies, waits for them, and re-layouts  46.5 us (4%)
  between operations  17.3 us (2%)
    unnamed x14, waiting for transfers between devices  145 us
    reduce_scatter x1, waiting for transfers between devices, body(): lax.psum_scatter(grad_fc, 'dp', scatter_dimension=0, tiled=True)  142 us
    reduce_scatter x1, waiting for transfers between devices, body(): lax.psum_scatter(grad_qkv, 'dp', scatter_dimension=0, tiled=True)  142 us
    unnamed x2, blocking collectives  117 us
    reduce_scatter x1, waiting for transfers between devices, body(): lax.psum_scatter(grad_dense, 'dp', scatter_dimension=0, tiled=True)  45 us
    all_gather x1, blocking collectives, body(): lax.all_gather(dense_weight, 'dp', axis=0, tiled=True)  44.1 us
    convert_element_type x4, other arithmetic, body(): grad_scores = (probs * (grad_probs - row_delta)).astype(jnp.bfloat16)  40.9 us
    dot_general x4, matrix products, body(): jnp.einsum('qhd,khd->hqk', heads_blk, value_low[:end_row], preferred_elem...  39.2 us
  transfers between devices with their start and end apart: 13, of which 4 were waited for; matrix products, arithmetic and copies ran while one was open for 37% of the time, Pallas kernels for 0%

profile of v1, /device:TPU:0, one launch (start us, length us, event | category | flops | bytes accessed | tf_op | source)
XLA Modules:
  0.0 1065.3 jit_solution(10863352786644890494)
XLA Ops:
  18.7 79.0 %all-reduce.26 = (bf16[768]{0:T(1024)(128)(2,1)S(1)}, bf16[768]{0:T(1024)(128)(2,1)S(1)}, bf16[3072]{0:T(1024)(128)(2,1)S(1)}, bf16[768]{0:T(1024)(128)(2,1)S(1)...) all-reduce(bf16[768]{0:T(1024)(128)(2,1)S(1)} %dynamic-update-slice, ...), channel_id=1, replica_groups=mesh['dp'=16,'tensor'=2] {'dp'}, use_global_device_ids=true, to_apply=%add.14 | all-reduce | flops 9984 | bytes 39936
  105.8 44.1 %all_gather.54 = bf16[768,6,64]{2,0,1:T(8,128)(2,1)S(1)} all-gather(bf16[48,6,64]{2,0,1:T(8,128)(2,1)S(1)} %copy-done.50), channel_id=1, replica_groups=mesh['dp'=16,'tensor'=2] {'dp'}, dimensions={0}, use_global_device_ids=true | all-gather | bytes 626688 | tf_op jit(solution)/shard_map/all_gather | solution.py:72
  211.7 8.4 fusion.153
  220.1 9.0 fusion.2
  229.1 12.9 %multiply_reduce_fusion.1 = (f32[6,512]{1,0:T(8,128)S(1)}, f32[6,512,1536]{2,1,0:T(8,128)}) fusion(f32[6,512,1536]{2,1,0:T(8,128)} %get-tuple-element.251, f32[6,512]{1,0:T(8,128)S(1)} %log_add_fusion.1, bf16[512,6,64]{0,2,1:T(8,128)(2,1)} %bitcast.137, bf16[2048,6,192]{0,2,1:T(8,128)(2,1)} %copy-done.9), kind=kOutput, calls=%fused_computation.10 | convolution fusion | flops 618132480 | bytes 39346176 | tf_op jit(solution)/shard_map/qhd,khd->hqk/dot_general | solution.py:235
  242.1 13.0 %multiply_convert_fusion.1 = bf16[6,512,1536]{2,1,0:T(8,128)(2,1)S(1)} fusion(f32[6,512,1536]{2,1,0:T(8,128)} %get-tuple-element.257, f32[6,512,1536]{2,1,0:T(8,128)} %get-tuple-element.251, f32[6,512]{1,0:T(8,128)S(1)} %get-tuple-element.256, f32[6,512]{1,0:T(8,128)S(1)} %log_add_fusion.1), kind=kLoop, calls=%fused_computation.9 | loop fusion | flops 18874368 | bytes 47210496 | tf_op jit(solution)/shard_map/convert_element_type | solution.py:239
  260.8 10.7 %fusion.154 = (f32[6,512]{1,0:T(8,128)S(1)}, f32[6,512,2048]{2,1,0:T(8,128)}) fusion(bf16[512,6,64]{0,2,1:T(8,128)(2,1)S(1)} %copy-done.32, bf16[2048,6,16]{0,2,1:T(8,128)(2,1)S(1)} %get-tuple-element.213, bf16[2048,6,48]{0,2,1:T(8,128)(2,1)S(1)} %get-tuple-element.219, pred[512,2048]{1,0:T(8,128)(4,1)S(1)} %copy-done.38), kind=kOutput, calls=%fused_computation.255 | convolution fusion | flops 827323392 | bytes 28192768 | tf_op jit(solution)/shard_map/qhd,khd->hqk/dot_general | solution.py:158
  271.5 10.5 fusion
  282.0 16.2 %multiply_reduce_fusion = (f32[6,512]{1,0:T(8,128)S(1)}, f32[6,512,2048]{2,1,0:T(8,128)}) fusion(f32[6,512,2048]{2,1,0:T(8,128)} %get-tuple-element.253, f32[6,512]{1,0:T(8,128)S(1)} %log_add_fusion, bf16[512,6,64]{0,2,1:T(8,128)(2,1)S(1)} %bitcast.135, bf16[2048,6,192]{0,2,1:T(8,128)(2,1)} %copy-done.9), kind=kOutput, calls=%fused_computation.1 | convolution fusion | flops 824177664 | bytes 52322304 | tf_op jit(solution)/shard_map/qhd,khd->hqk/dot_general | solution.py:235
  298.2 17.0 %multiply_convert_fusion = bf16[6,512,2048]{2,1,0:T(8,128)(2,1)S(1)} fusion(f32[6,512,2048]{2,1,0:T(8,128)} %get-tuple-element.255, f32[6,512,2048]{2,1,0:T(8,128)} %get-tuple-element.253, f32[6,512]{1,0:T(8,128)S(1)} %get-tuple-element.254, f32[6,512]{1,0:T(8,128)S(1)} %log_add_fusion), kind=kLoop, calls=%fused_computation | loop fusion | flops 25165824 | bytes 62939136 | tf_op jit(solution)/shard_map/convert_element_type | solution.py:239
  325.8 8.0 bitcast_add_fusion.2
  355.8 11.6 %bitcast_add_fusion.1 = bf16[2048,6,64]{0,2,1:T(8,128)(2,1)S(1)} fusion(f32[2048,6,64]{0,2,1:T(8,128)} %fusion.68, bf16[512,6,64]{0,2,1:T(8,128)(2,1)S(1)} %bitcast.136, f32[6,512,2048]{2,1,0:T(8,128)} %get-tuple-element.253, f32[6,512]{1,0:T(8,128)S(1)} %log_add_fusion), kind=kOutput, calls=%fused_computation.109 | convolution fusion | flops 819462144 | bytes 30289920 | tf_op jit(solution)/shard_map/hqk,qhd->khd/dot_general | solution.py:256
  382.5 9.3 fusion.105
  392.5 34.9 %multiply_convert_fusion.3 = (bf16[2048,1536]{1,0:T(8,128)(2,1)}, f32[2048,1536]{1,0:T(8,128)}, f32[2048,1536]{1,0:T(8,128)}) fusion(f32[1536]{0:T(1024)S(1)} %copy-done.64, bf16[2048,768]{1,0:T(8,128)(2,1)} %all-gather.11.cloned.1.call-done, bf16[768,1536]{1,0:T(8,128)(2,1)} %all-gather.13.cloned.1.call-done), kind=kOutput, calls=%fused_computation.25 | convolution fusion | flops 5039456256 | bytes 36968448 | tf_op jit(solution)/shard_map/dot_general | solution.py:195
  427.3 17.0 %convert_reduce_fusion = (f32[1536]{0:T(1024)S(1)}, bf16[2048,1536]{1,0:T(8,128)(2,1)S(1)}) fusion(f32[2048,1536]{1,0:T(8,128)} %get-tuple-element.212, bf16[2048,768]{1,0:T(8,128)(2,1)} %all-gather.17.cloned.1.call-done, bf16[768,1536]{1,0:T(8,128)(2,1)} %all-gather.15.cloned.1.call-done, f32[2048,1536]{1,0:T(8,128)} %get-tuple-element.245, ...), kind=kOutput, calls=%fused_computation.19 | convolution fusion | flops 4885314048 | bytes 36974592 | tf_op jit(solution)/shard_map/dot_general | solution.py:212
  466.0 11.1 %fusion.106 = bf16[6,64,512]{2,1,0:T(8,128)(2,1)S(1)} fusion(f32[6,512,2048]{2,1,0:T(8,128)} %get-tuple-element.253, f32[6,512]{1,0:T(8,128)S(1)} %copy-done.60, f32[6,512]{1,0:T(8,128)S(1)} %copy-done.58, bf16[2048,6,192]{0,2,1:T(8,128)(2,1)} %copy-done.9), kind=kOutput, calls=%fused_computation.174 | convolution fusion | flops 824377344 | bytes 27156480 | tf_op jit(solution)/shard_map/hqk,khd->qhd/dot_general | solution.py:182
  494.4 10.0 fusion.33
  504.5 9.8 fusion.156
  514.4 9.7 convolution_bitcast_fusion
  545.5 37.7 %all-reduce.25 = (f32[768]{0:T(1024)S(1)}, f32[768]{0:T(1024)S(1)}, f32[768]{0:T(1024)S(1)}, f32[768]{0:T(1024)S(1)}, f32[2304]{0:T(1024)S(1)}, /*index=5*/f32[768]{0:T(1024)S(1)}, f32[3072]{0:T(1024)S(1)}) all-reduce(f32[768]{0:T(1024)S(1)} %get-tuple-element.187, ...), channel_id=5, replica_groups=mesh['dp'=16,'tensor'=2] {'dp','tensor'}, use_global_device_ids=true, to_apply=%region_25.26.clone | all-reduce | flops 9216 | bytes 73728
  586.8 45.0 %reduce-scatter.18.cloned.1.call-done = f32[48,6,64]{2,0,1:T(8,128)} async-done(((f32[768,6,64]{2,0,1:T(8,128)}), f32[48,6,64]{2,0,1:T(8,128)}) %reduce-scatter.18.cloned.1.call-update) | async-done | bytes 73744 | tf_op jit(solution)/shard_map/reduce_scatter | solution.py:317
  631.8 141.7 %reduce-scatter.16.cloned.1.call-done = f32[48,6,192]{2,0,1:T(8,128)} async-done(((f32[768,6,192]{2,0,1:T(8,128)}), f32[48,6,192]{2,0,1:T(8,128)}) %reduce-scatter.16.cloned.1.call-update) | async-done | bytes 221200 | tf_op jit(solution)/shard_map/reduce_scatter | solution.py:316
  773.5 142.4 %reduce-scatter.20.cloned.1.call-done = f32[48,1536]{1,0:T(8,128)} async-done(((f32[768,1536]{1,0:T(8,128)}), f32[48,1536]{1,0:T(8,128)}) %reduce-scatter.20.cloned.1.call-update) | async-done | bytes 294928 | tf_op jit(solution)/shard_map/reduce_scatter | solution.py:318
  915.9 142.2 %reduce-scatter.22.cloned.1.call-done = f32[48,1536]{1,0:T(8,128)} async-done(((f32[768,1536]{1,0:T(8,128)}), f32[48,1536]{1,0:T(8,128)}) %reduce-scatter.22.cloned.1.call-update) | async-done | bytes 294928
  (322 shorter events, 196.8 us)
Async XLA Ops:
  7.2 92.2 %copy-start.3 = (bf16[1024,768]{1,0:T(8,128)(2,1)S(1)}, bf16[1024,768]{1,0:T(8,128)(2,1)}, u32[]{:S(2)}) copy-start(bf16[1024,768]{1,0:T(8,128)(2,1)} %param.35) | copy-start | bytes 4718596
  7.2 149.9 %all-gather.17.cloned.1.call-start = ((), (), s32[]{:S(2)}) async-start(), calls=%async_computation.13 | async-start | bytes 4718592 | tf_op jit(solution)/shard_map/all_gather | solution.py:211
  7.9 153.8 %all-gather.9.cloned.1.call-start = ((), (), s32[]{:S(2)}) async-start(), calls=%async_computation.8 | async-start | bytes 2506752 | tf_op jit(solution)/shard_map/all_gather | solution.py:71
  8.7 156.3 %all-gather.7.cloned.1.call-start = ((), (), s32[]{:S(2)}) async-start(), calls=%async_computation.7 | async-start | bytes 4718592 | tf_op jit(solution)/shard_map/all_gather | solution.py:125
  103.2 288.6 %all-gather.11.cloned.1.call-start = ((), (), s32[]{:S(2)}) async-start(), calls=%async_computation.9 | async-start | bytes 4718592 | tf_op jit(solution)/shard_map/all_gather | solution.py:126
  103.8 288.1 %all-gather.13.cloned.1.call-start = ((), (), s32[]{:S(2)}) async-start(), calls=%async_computation.10 | async-start | bytes 2506752 | tf_op jit(solution)/shard_map/all_gather | solution.py:73
  104.4 322.9 %all-gather.15.cloned.1.call-start = ((), (), s32[]{:S(2)}) async-start(), calls=%async_computation.11 | async-start | bytes 2506752 | tf_op jit(solution)/shard_map/all_gather | solution.py:74
  105.0 426.6 %reduce-scatter.14.cloned.1.call-start = ((), (), s32[]{:S(2)}) async-start(), calls=%async_computation.15 | async-start | bytes 4718592 | tf_op jit(solution)/shard_map/reduce_scatter | solution.py:282
  105.8 66.1 %copy-start.33 = (f32[2048,16]{0,1:T(8,128)}, f32[2048,16]{0,1:T(8,128)S(1)}, u32[]{:S(2)}) copy-start(f32[2048,16]{0,1:T(8,128)S(1)} %get-tuple-element.237) | copy-start | bytes 393220
  105.8 66.1 %copy-start.35 = (f32[2048,16]{0,1:T(8,128)}, f32[2048,16]{0,1:T(8,128)S(1)}, u32[]{:S(2)}) copy-start(f32[2048,16]{0,1:T(8,128)S(1)} %get-tuple-element.238) | copy-start | bytes 393220
  171.7 22.8 %copy-start.9 = (bf16[2048,6,192]{0,2,1:T(8,128)(2,1)}, bf16[2048,6,192]{0,2,1:T(8,128)(2,1)S(1)}, u32[]{:S(2)}) copy-start(bf16[2048,6,192]{0,2,1:T(8,128)(2,1)S(1)} %convert.33) | copy-start | bytes 14155780
  171.9 88.8 %copy-start.5 = (bf16[2048,6,48]{0,2,1:T(8,128)(2,1)}, bf16[2048,6,48]{0,2,1:T(8,128)(2,1)S(1)}, u32[]{:S(2)}) copy-start(bf16[2048,6,48]{0,2,1:T(8,128)(2,1)S(1)} %get-tuple-element.219) | copy-start | bytes 3538948
  325.8 18.1 %slice-start = ((s8[12582912]{0:T(1024)(128)(4,1)}), s8[4194304]{0:T(1024)(128)(4,1)S(1)}, s32[]{:S(2)}) async-start(s8[12582912]{0:T(1024)(128)(4,1)} %bitcast.128), calls=%async_computation.20 | async-start | bytes 8388608
  325.8 18.1 %slice-start.1 = ((s8[12582912]{0:T(1024)(128)(4,1)}), s8[4194304]{0:T(1024)(128)(4,1)S(1)}, s32[]{:S(2)}) async-start(s8[12582912]{0:T(1024)(128)(4,1)} %bitcast.128), calls=%async_computation.21 | async-start | bytes 8388608
  325.8 23.6 %slice-start.3 = ((s8[18874368]{0:T(1024)(128)(4,1)}), s8[4194304]{0:T(1024)(128)(4,1)S(1)}, s32[]{:S(2)}) async-start(s8[18874368]{0:T(1024)(128)(4,1)} %bitcast.130), calls=%async_computation.23 | async-start | bytes 8388608
  325.8 23.6 %slice-start.4 = ((s8[18874368]{0:T(1024)(128)(4,1)}), s8[4194304]{0:T(1024)(128)(4,1)S(1)}, s32[]{:S(2)}) async-start(s8[18874368]{0:T(1024)(128)(4,1)} %bitcast.130), calls=%async_computation.24 | async-start | bytes 8388608
  391.8 139.8 %reduce-scatter.12.cloned.1.call-start = ((), (), s32[]{:S(2)}) async-start(), calls=%async_computation.14 | async-start | bytes 4718592 | tf_op jit(solution)/shard_map/reduce_scatter | solution.py:285
  427.3 19.6 %copy-start.68 = (bf16[768,1536]{1,0:T(8,128)(2,1)S(1)}, bf16[768,1536]{1,0:T(8,128)(2,1)}, u32[]{:S(2)}) copy-start(bf16[768,1536]{1,0:T(8,128)(2,1)} %all-gather.13.cloned.1.call-done) | copy-start | bytes 7077892
  453.4 85.6 %reduce-scatter.10.cloned.1.call-start = ((), (), s32[]{:S(2)}) async-start(), calls=%async_computation.12 | async-start | bytes 4718592 | tf_op jit(solution)/shard_map/reduce_scatter | solution.py:199
  489.1 142.7 %reduce-scatter.18.cloned.1.call-start = ((), (), s32[]{:S(2)}) async-start(), calls=%async_computation.17 | async-start | bytes 2506752 | tf_op jit(solution)/shard_map/reduce_scatter | solution.py:317
  494.4 279.2 %reduce-scatter.16.cloned.1.call-start = ((), (), s32[]{:S(2)}) async-start(), calls=%async_computation.16 | async-start | bytes 5013504 | tf_op jit(solution)/shard_map/reduce_scatter | solution.py:316
  504.4 411.5 %reduce-scatter.20.cloned.1.call-start = ((), (), s32[]{:S(2)}) async-start(), calls=%async_computation.18 | async-start | bytes 5013504 | tf_op jit(solution)/shard_map/reduce_scatter | solution.py:318
  514.4 543.8 %reduce-scatter.22.cloned.1.call-start = ((), (), s32[]{:S(2)}) async-start(), calls=%async_computation.19 | async-start | bytes 5013504
  583.9 474.8 %copy-start.71 = (f32[24]{0:T(128)}, f32[24]{0:T(128)S(1)}, u32[]{:S(2)}) copy-start(f32[24]{0:T(128)S(1)} %dynamic-slice.72) | copy-start | bytes 292
  (72 other events, 337.2 us)
Sparse Core Ops, SparseCore 0:
  9.6 14.8 all-gather.16
  27.1 64.0 all-gather.8
  103.4 7.9 all-gather.6
  112.8 13.2 all-gather.10
  128.8 64.0 all-gather.12
  195.5 61.1 all-gather.14
  391.9 8.2 reduce-scatter.13
  453.5 8.2 reduce-scatter.11
  489.2 7.7 reduce-scatter.9
  503.1 128.6 reduce-scatter.17
  637.6 135.9 reduce-scatter.15
  780.0 135.9 reduce-scatter.19
  921.7 136.4 reduce-scatter.21

commit v2 on v1

--- a/solution.py
+++ b/solution.py
@@ -15,6 +15,51 @@
     owner_mask = seg_ids[:, None] == jnp.arange(lengths.shape[0], dtype=jnp.int32)[None, :]
     positions = row_index - jnp.sum(jnp.where(owner_mask, starts[None, :], 0), axis=1)
     return (seg_ids, positions)
+
+
+def steps_from(size, turn):
+    steps = []
+    step = 1
+    while step < size:
+        steps.append(step)
+        step *= 2
+    return steps[turn:] + steps[:turn]
+
+
+def exchange(values, axis, step):
+    size = lax.axis_size(axis)
+    return lax.ppermute(values, axis, [(i, i ^ step) for i in range(size)])
+
+
+def gather_pairs(block, axis, turn=0):
+    size = lax.axis_size(axis)
+    index = lax.axis_index(axis)
+    order = steps_from(size, turn)[::-1]
+    held = block
+    for step in order:
+        other = exchange(held, axis, step)
+        is_low = (index // step) % 2 == 0
+        held = jnp.stack([jnp.where(is_low, held, other), jnp.where(is_low, other, held)])
+    placed = order[::-1]
+    want = sorted(placed, reverse=True)
+    tail = range(len(order), held.ndim)
+    held = held.transpose([placed.index(step) for step in want] + list(tail))
+    return held.reshape((size * block.shape[0],) + block.shape[1:])
+
+
+def scatter_pairs(full, axis, turn=0, sent=jnp.bfloat16):
+    size = lax.axis_size(axis)
+    index = lax.axis_index(axis)
+    left = sorted(steps_from(size, 0), reverse=True)
+    held = full.reshape([2] * len(left) + [full.shape[0] // size] + list(full.shape[1:]))
+    for step in steps_from(size, turn):
+        spot = left.index(step)
+        bit = (index // step) % 2
+        away = lax.dynamic_index_in_dim(held, 1 - bit, spot, keepdims=False).astype(sent)
+        kept = lax.dynamic_index_in_dim(held, bit, spot, keepdims=False).astype(jnp.float32)
+        held = kept + exchange(away, axis, step).astype(jnp.float32)
+        left.remove(step)
+    return held
 
 
 def layer_norm(values, gain_vec, shift_vec):
@@ -67,25 +112,25 @@
     tensor_count = lax.axis_size("tensor")
     local_rows = hidden_in.shape[0]
     group_rows = local_rows * tensor_count
-    gathered = (
-        lax.all_gather(qkv_weight, "dp", axis=0, tiled=True),
-        lax.all_gather(dense_weight, "dp", axis=0, tiled=True),
-        lax.all_gather(fc_weight, "dp", axis=0, tiled=True),
-        lax.all_gather(proj_weight, "dp", axis=0, tiled=True),
-        lax.all_gather(attn_gain, "dp", axis=0, tiled=True),
-        lax.all_gather(attn_shift, "dp", axis=0, tiled=True),
-        lax.all_gather(mlp_gain, "dp", axis=0, tiled=True),
-        lax.all_gather(mlp_shift, "dp", axis=0, tiled=True),
-        lax.all_gather(qkv_bias, "dp", axis=0, tiled=True),
-        lax.all_gather(dense_bias, "dp", axis=0, tiled=True),
-        lax.all_gather(fc_bias, "dp", axis=0, tiled=True),
-        lax.all_gather(proj_bias, "dp", axis=0, tiled=True),
-    )
+    rows_all = gather_pairs(hidden_in, "tensor")
+    cot_all = gather_pairs(out_grad, "tensor")
+    smalls = (
+        attn_gain,
+        attn_shift,
+        mlp_gain,
+        mlp_shift,
+        qkv_bias,
+        dense_bias,
+        fc_bias,
+        proj_bias,
+    )
+    packed = gather_pairs(jnp.concatenate(smalls)[None], "dp", 0)
+    parts = []
+    begin = 0
+    for item in smalls:
+        parts.append(packed[:, begin : begin + item.shape[0]].reshape(-1))
+        begin += item.shape[0]
     (
-        w_qkv,
-        w_dense,
-        w_fc,
-        w_proj,
         gain_attn,
         shift_attn,
         gain_mlp,
@@ -94,11 +139,14 @@
         bias_dense,
         bias_fc,
         bias_proj,
-    ) = gathered
+    ) = parts
+    head_count, triple_width = qkv_weight.shape[1:]
+    w_qkv = gather_pairs(qkv_weight.reshape(qkv_weight.shape[0], -1), "dp", 2)
+    w_dense = gather_pairs(dense_weight.reshape(dense_weight.shape[0], -1), "dp", 2)
+    w_fc = gather_pairs(fc_weight, "dp", 0)
+    w_proj = gather_pairs(proj_weight, "dp", 1)
     model_width = w_qkv.shape[0]
-    head_count = w_qkv.shape[1]
-    triple_width = w_qkv.shape[2]
-    head_dim = w_dense.shape[2]
+    head_dim = dense_weight.shape[2]
     hidden_units = w_fc.shape[1]
     qkv_cols = head_count * triple_width
     attn_cols = head_count * head_dim
@@ -118,16 +166,18 @@
     def norms(values, gain_one, shift_one, gain_two, shift_two):
         return (layer_norm(values, gain_one, shift_one), layer_norm(values, gain_two, shift_two))
 
-    (normed_one, normed_two), norm_back = jax.vjp(
+    _, norm_back = jax.vjp(
         norms, x_rows, gain_attn_f, shift_attn_f, gain_mlp_f, shift_mlp_f
     )
     normed_attn, normed_mlp = (
-        lax.all_gather(normed_one.astype(jnp.bfloat16), "tensor", axis=0, tiled=True),
-        lax.all_gather(normed_two.astype(jnp.bfloat16), "tensor", axis=0, tiled=True),
+        normed.astype(jnp.bfloat16)
+        for normed in norms(
+            rows_all.astype(jnp.float32), gain_attn_f, shift_attn_f, gain_mlp_f, shift_mlp_f
+        )
     )
     merged_lin = (
         jnp.dot(
-            normed_attn, w_qkv.reshape(model_width, qkv_cols), preferred_element_type=jnp.float32
+            normed_attn, w_qkv, preferred_element_type=jnp.float32
         )
         + my_bias_qkv
     )
@@ -189,41 +239,31 @@
     attn_part = jnp.einsum(
         "gc,dc->gd",
         heads_flat,
-        w_dense.reshape(model_width, attn_cols),
+        w_dense,
         preferred_element_type=jnp.float32,
     )
     fc_pre = jnp.dot(normed_mlp, w_fc, preferred_element_type=jnp.float32) + my_bias_fc
     act_full, gelu_back = jax.vjp(exact_gelu, fc_pre)
     act_low = act_full.astype(jnp.bfloat16)
     mlp_part = jnp.einsum("gf,df->gd", act_low, w_proj, preferred_element_type=jnp.float32)
-    branch_rows = lax.psum_scatter(
-        (attn_part + mlp_part).astype(jnp.bfloat16), "tensor", scatter_dimension=0, tiled=True
-    ).astype(jnp.float32)
+    branch_rows = scatter_pairs(attn_part + mlp_part, "tensor")
     block_out = (
         x_rows + branch_rows + bias_dense.astype(jnp.float32) + bias_proj.astype(jnp.float32)
     ).astype(jnp.bfloat16)
-    w_qkv, w_dense, w_fc, w_proj = (
-        lax.all_gather(qkv_weight, "dp", axis=0, tiled=True),
-        lax.all_gather(dense_weight, "dp", axis=0, tiled=True),
-        lax.all_gather(fc_weight, "dp", axis=0, tiled=True),
-        lax.all_gather(proj_weight, "dp", axis=0, tiled=True),
-    )
-    cot_all = lax.all_gather(out_grad, "tensor", axis=0, tiled=True)
     grad_act = jnp.dot(cot_all, w_proj, preferred_element_type=jnp.float32)
     grad_proj = jnp.einsum("gd,gf->df", cot_all, act_low, preferred_element_type=jnp.float32)
     grad_pre = gelu_back(grad_act)[0].astype(jnp.bfloat16)
     grad_fc = jnp.einsum("gd,gf->df", normed_mlp, grad_pre, preferred_element_type=jnp.float32)
     fc_bias_part = jnp.sum(grad_pre, axis=0, dtype=jnp.float32)
     grad_normed_mlp = jnp.einsum("gf,df->gd", grad_pre, w_fc, preferred_element_type=jnp.float32)
-    dense_flat = w_dense.reshape(model_width, attn_cols)
     grad_heads = (
-        jnp.dot(cot_all, dense_flat, preferred_element_type=jnp.float32)
+        jnp.dot(cot_all, w_dense, preferred_element_type=jnp.float32)
         .astype(jnp.bfloat16)
         .reshape(group_rows, head_count, head_dim)
     )
     grad_dense = jnp.einsum(
         "gd,gc->dc", cot_all, heads_flat, preferred_element_type=jnp.float32
-    ).reshape(model_width, head_count, head_dim)
+    )
     query_grads = []
     grad_key = jnp.zeros((group_rows, head_count, head_dim), jnp.float32)
     grad_value = jnp.zeros((group_rows, head_count, head_dim), jnp.float32)
@@ -269,22 +309,18 @@
     )
     grad_qkv = jnp.einsum(
         "gd,gc->dc", normed_attn, grad_merged, preferred_element_type=jnp.float32
-    ).reshape(model_width, head_count, triple_width)
+    )
     qkv_bias_part = jnp.sum(grad_merged, axis=0, dtype=jnp.float32)
     grad_normed_attn = jnp.einsum(
         "gc,dc->gd",
         grad_merged,
-        w_qkv.reshape(model_width, qkv_cols),
+        w_qkv,
         preferred_element_type=jnp.float32,
     )
     cot_rows = out_grad.astype(jnp.float32)
     local_attn, local_mlp = (
-        lax.psum_scatter(
-            grad_normed_attn.astype(jnp.bfloat16), "tensor", scatter_dimension=0, tiled=True
-        ).astype(jnp.float32),
-        lax.psum_scatter(
-            grad_normed_mlp.astype(jnp.bfloat16), "tensor", scatter_dimension=0, tiled=True
-        ).astype(jnp.float32),
+        scatter_pairs(grad_normed_attn, "tensor"),
+        scatter_pairs(grad_normed_mlp, "tensor"),
     )
     grad_x, grad_gain_attn, grad_shift_attn, grad_gain_mlp, grad_shift_mlp = norm_back(
         (local_attn, local_mlp)
@@ -303,20 +339,38 @@
         tensor_index * hidden_units,
         0,
     )
-    small_sums = (
-        lax.psum_scatter(grad_gain_attn, ("dp", "tensor"), scatter_dimension=0, tiled=True),
-        lax.psum_scatter(grad_shift_attn, ("dp", "tensor"), scatter_dimension=0, tiled=True),
-        lax.psum_scatter(grad_gain_mlp, ("dp", "tensor"), scatter_dimension=0, tiled=True),
-        lax.psum_scatter(grad_shift_mlp, ("dp", "tensor"), scatter_dimension=0, tiled=True),
-        lax.psum_scatter(full_qkv_bias, ("dp", "tensor"), scatter_dimension=0, tiled=True),
-        lax.psum_scatter(cot_sums, ("dp", "tensor"), scatter_dimension=0, tiled=True),
-        lax.psum_scatter(full_fc_bias, ("dp", "tensor"), scatter_dimension=0, tiled=True),
+    owners = lax.axis_size("dp") * tensor_count
+    small_list = (
+        grad_gain_attn,
+        grad_shift_attn,
+        grad_gain_mlp,
+        grad_shift_mlp,
+        full_qkv_bias,
+        cot_sums,
+        full_fc_bias,
+    )
+    small_packed = jnp.concatenate([item.reshape(owners, -1) for item in small_list], axis=1)
+    small_packed = scatter_pairs(small_packed, "dp", 0, jnp.float32)
+    small_packed = scatter_pairs(small_packed, "tensor", 0, jnp.float32).reshape(-1)
+    small_sums = []
+    begin = 0
+    for item in small_list:
+        count = item.shape[0] // owners
+        small_sums.append(small_packed[begin : begin + count])
+        begin += count
+    third = qkv_cols // 3
+    sum_qkv = jnp.concatenate(
+        [
+            scatter_pairs(grad_qkv[:, turn * third : (turn + 1) * third], "dp", turn)
+            for turn in range(3)
+        ],
+        axis=1,
     )
     large_sums = (
-        lax.psum_scatter(grad_qkv, "dp", scatter_dimension=0, tiled=True),
-        lax.psum_scatter(grad_dense, "dp", scatter_dimension=0, tiled=True),
-        lax.psum_scatter(grad_fc, "dp", scatter_dimension=0, tiled=True),
-        lax.psum_scatter(grad_proj, "dp", scatter_dimension=0, tiled=True),
+        sum_qkv.reshape(qkv_weight.shape),
+        scatter_pairs(grad_dense, "dp", 2).reshape(dense_weight.shape),
+        scatter_pairs(grad_fc, "dp", 1),
+        scatter_pairs(grad_proj, "dp", 2),
     )
     return (
         block_out,

time: 1070 us -> 667 us (0.62)
  waiting for transfers between devices: 475 us -> 147 us
  blocking collectives: 161 us -> 0 us
  starting transfers between devices: 0.52 us -> 51.7 us
  local copies, waits for them, and re-layouts: 46.5 us -> 81.6 us
  other arithmetic: 101 us -> 132 us
  matrix products: 264 us -> 245 us
  between operations: 17.3 us -> 2.99 us
    reduce_scatter x6 -> x0, waiting for transfers between devices: 329 us -> none  [the longest x1 142 us: body(): lax.psum_scatter(grad_fc, 'dp', scatter_dimension=0, tiled=True)]
    ppermute x0 -> x54, waiting for transfers between devices: none -> 147 us  [exchange(): return lax.ppermute(values, axis, [(i, i ^ step) for i in range(size)])]
    unnamed x14 -> x0, waiting for transfers between devices: 145 us -> none
    unnamed x2 -> x0, blocking collectives: 117 us -> none
    ppermute x0 -> x54, starting transfers between devices: none -> 51.7 us  [exchange(): return lax.ppermute(values, axis, [(i, i ^ step) for i in range(size)])]
    all_gather x1 -> x0, blocking collectives: 44.1 us -> none  [body(): lax.all_gather(dense_weight, 'dp', axis=0, tiled=True)]
    convert_element_type x0 -> x34, local copies, waits for them, and re-layouts: none -> 22.9 us  [the longest x27 12.3 us: scatter_pairs(): lax.dynamic_index_in_dim(held, 1 - bit, spot, keepdims=False).astype(sent)]
    another operation x2 -> x43, other arithmetic: 1.03 us -> 14.9 us  [the longest x39 13.4 us: gather_pairs(): jnp.stack([jnp.where(is_low, held, other), jnp.where(is_low, other, held)])]
  transfers between devices with their start and end apart: 13 -> 54, of which waited for: 4 -> 28; matrix products, arithmetic and copies ran while one was open for 37% -> 65% of each run, Pallas kernels for 0% -> 0%
where the time goes in v2:
time: 667 us; the launch traced here: 659 us
  matrix products  245 us (37%)
  waiting for transfers between devices  147 us (22%)
  other arithmetic  132 us (20%)
  local copies, waits for them, and re-layouts  81.6 us (12%)
  starting transfers between devices  51.7 us (8%)
    ppermute x54, waiting for transfers between devices, exchange(): return lax.ppermute(values, axis, [(i, i ^ step) for i in range(size)])  147 us
    ppermute x54, starting transfers between devices, exchange(): return lax.ppermute(values, axis, [(i, i ^ step) for i in range(size)])  51.7 us
    dot_general x4, matrix products, body(): jnp.einsum('qhd,khd->hqk', heads_blk, value_low[:end_row], preferred_elem...  44 us
    convert_element_type x4, other arithmetic, body(): grad_scores = (probs * (grad_probs - row_delta)).astype(jnp.bfloat16)  40.5 us
    dot_general x1, matrix products, body(): jnp.dot(normed_mlp, w_fc, preferred_element_type=jnp.float32) + my_bias_fc  32.8 us
    dot_general x4, matrix products, body(): jnp.einsum('hqk,qhd->khd', probs.astype(jnp.bfloat16), heads_blk, preferr...  28.1 us
    dot_general x4, matrix products, body(): jnp.einsum('hqk,khd->qhd', prob_low, value_low[:end_row], preferred_eleme...  27 us
    unnamed x191, local copies, waits for them, and re-layouts  26 us
  transfers between devices with their start and end apart: 54, of which 28 were waited for; matrix products, arithmetic and copies ran while one was open for 65% of the time, Pallas kernels for 0%

profile of v2, /device:TPU:0, one launch (start us, length us, event | category | flops | bytes accessed | tf_op | source)
XLA Modules:
  0.0 659.3 jit_solution(14010799092077724628)
XLA Ops:
  59.6 20.6 %collective-permute-done.18 = bf16[2,48,1536]{2,1,0:T(8,128)(2,1)S(1)} collective-permute-done((bf16[2,48,1536]{2,1,0:T(8,128)(2,1)S(1)}, bf16[2,48,1536]{2,1,0:T(8,128)(2,1)S(1)}, u32[]{:S(2)}, u32[]{:S(2)}) %collective-permute-start.18) | collective-permute-done | bytes 294944 | tf_op jit(solution)/shard_map/ppermute | solution.py:31
  82.2 6.9 %collective-permute-done.7 = bf16[2,2,48,1152]{3,2,1,0:T(8,128)(2,1)S(1)} collective-permute-done((bf16[2,2,48,1152]{3,2,1,0:T(8,128)(2,1)S(1)}, bf16[2,2,48,1152]{3,2,1,0:T(8,128)(2,1)S(1)}, u32[]{:S(2)}, u32[]{:S(2)}) %collective-permute-start.7) | collective-permute-done | bytes 442400 | tf_op jit(solution)/shard_map/ppermute | solution.py:31
  166.2 8.3 %fusion.191 = (f32[6,512]{1,0:T(8,128)S(1)}, f32[6,512,1536]{2,1,0:T(8,128)}) fusion(bf16[2048,6,48]{0,2,1:T(8,128)(2,1)S(1)} %get-tuple-element.221, bf16[2048,6,16]{0,2,1:T(8,128)(2,1)S(1)} %get-tuple-element.215, bf16[2048,6,48]{0,2,1:T(8,128)(2,1)S(1)} %get-tuple-element.222, bf16[2048,6,16]{0,2,1:T(8,128)(2,1)S(1)} %get-tuple-element.216, ...), kind=kOutput, calls=%fused_computation.443 | convolution fusion | flops 621278208 | bytes 22818816 | tf_op jit(solution)/shard_map/qhd,khd->hqk/dot_general | solution.py:208
  174.5 9.0 %fusion.2 = f32[6,512]{1,0:T(8,128)S(1)} fusion(f32[6,512,1536]{2,1,0:T(8,128)} %get-tuple-element.316, f32[6,512]{1,0:T(8,128)S(1)} %get-tuple-element.315), kind=kLoop, calls=%fused_computation.15 | loop fusion | flops 9434112 | bytes 18898944 | tf_op jit(solution)/shard_map/reduce_sum | solution.py:228
  183.5 9.4 %fusion.94 = bf16[6,64,512]{2,1,0:T(8,128)(2,1)} fusion(f32[6,512,1536]{2,1,0:T(8,128)} %get-tuple-element.316, f32[6,512]{1,0:T(8,128)S(1)} %fusion.2, f32[6,512]{1,0:T(8,128)S(1)} %get-tuple-element.315, bf16[2048,6,192]{0,2,1:T(8,128)(2,1)} %copy-done.7), kind=kOutput, calls=%fused_computation.178 | convolution fusion | flops 618332160 | bytes 20471808 | tf_op jit(solution)/shard_map/hqk,khd->qhd/dot_general | solution.py:232
  192.9 10.7 %fusion.192 = (f32[6,512]{1,0:T(8,128)S(1)}, f32[6,512,2048]{2,1,0:T(8,128)}) fusion(bf16[512,6,64]{0,2,1:T(8,128)(2,1)S(1)} %copy-done.58, bf16[2048,6,16]{0,2,1:T(8,128)(2,1)S(1)} %get-tuple-element.215, bf16[2048,6,48]{0,2,1:T(8,128)(2,1)S(1)} %get-tuple-element.221, pred[512,2048]{1,0:T(8,128)(4,1)S(1)} %copy-done.64), kind=kOutput, calls=%fused_computation.444 | convolution fusion | flops 827323392 | bytes 28192768 | tf_op jit(solution)/shard_map/qhd,khd->hqk/dot_general | solution.py:208
  203.7 10.4 %fusion = f32[6,512]{1,0:T(8,128)S(1)} fusion(f32[6,512,2048]{2,1,0:T(8,128)} %get-tuple-element.318, f32[6,512]{1,0:T(8,128)S(1)} %get-tuple-element.317), kind=kLoop, calls=%fused_computation.6 | loop fusion | flops 12579840 | bytes 25190400 | tf_op jit(solution)/shard_map/reduce_sum | solution.py:228
  214.1 11.9 %fusion.95 = bf16[6,64,512]{2,1,0:T(8,128)(2,1)} fusion(f32[6,512,2048]{2,1,0:T(8,128)} %get-tuple-element.318, f32[6,512]{1,0:T(8,128)S(1)} %fusion, f32[6,512]{1,0:T(8,128)S(1)} %get-tuple-element.317, bf16[2048,6,192]{0,2,1:T(8,128)(2,1)} %copy-done.7), kind=kOutput, calls=%fused_computation.179 | convolution fusion | flops 824377344 | bytes 27156480 | tf_op jit(solution)/shard_map/hqk,khd->qhd/dot_general | solution.py:232
  226.0 10.9 %multiply_reduce_fusion.2 = (f32[6,512]{1,0:T(8,128)S(1)}, f32[6,512,1024]{2,1,0:T(8,128)}) fusion(f32[6,512,1024]{2,1,0:T(8,128)} %copy-done, f32[6,512]{1,0:T(8,128)S(1)} %log_add_fusion.2, bf16[512,6,64]{0,2,1:T(8,128)(2,1)S(1)} %bitcast.457, bf16[2048,6,192]{0,2,1:T(8,128)(2,1)} %copy-done.7), kind=kOutput, calls=%fused_computation.22 | convolution fusion | flops 412087296 | bytes 26370048 | tf_op jit(solution)/shard_map/qhd,khd->hqk/dot_general | solution.py:275
  249.8 13.0 %multiply_reduce_fusion.1 = (f32[6,512]{1,0:T(8,128)S(1)}, f32[6,512,1536]{2,1,0:T(8,128)}) fusion(f32[6,512,1536]{2,1,0:T(8,128)} %get-tuple-element.316, f32[6,512]{1,0:T(8,128)S(1)} %log_add_fusion.1, bf16[512,6,64]{0,2,1:T(8,128)(2,1)S(1)} %bitcast.454, bf16[2048,6,192]{0,2,1:T(8,128)(2,1)} %copy-done.7), kind=kOutput, calls=%fused_computation.10 | convolution fusion | flops 618132480 | bytes 39346176 | tf_op jit(solution)/shard_map/qhd,khd->hqk/dot_general | solution.py:275
  262.8 12.9 %multiply_convert_fusion.1 = bf16[6,512,1536]{2,1,0:T(8,128)(2,1)S(1)} fusion(f32[6,512,1536]{2,1,0:T(8,128)} %get-tuple-element.322, f32[6,512,1536]{2,1,0:T(8,128)} %get-tuple-element.316, f32[6,512]{1,0:T(8,128)S(1)} %get-tuple-element.321, f32[6,512]{1,0:T(8,128)S(1)} %log_add_fusion.1), kind=kLoop, calls=%fused_computation.9 | loop fusion | flops 18874368 | bytes 47210496 | tf_op jit(solution)/shard_map/convert_element_type | solution.py:279
  282.9 16.2 %multiply_reduce_fusion = (f32[6,512]{1,0:T(8,128)S(1)}, f32[6,512,2048]{2,1,0:T(8,128)}) fusion(f32[6,512,2048]{2,1,0:T(8,128)} %get-tuple-element.318, f32[6,512]{1,0:T(8,128)S(1)} %log_add_fusion, bf16[512,6,64]{0,2,1:T(8,128)(2,1)S(1)} %bitcast.451, bf16[2048,6,192]{0,2,1:T(8,128)(2,1)} %copy-done.7), kind=kOutput, calls=%fused_computation.1 | convolution fusion | flops 824177664 | bytes 52322304 | tf_op jit(solution)/shard_map/qhd,khd->hqk/dot_general | solution.py:275
  299.1 16.7 %multiply_convert_fusion = bf16[6,512,2048]{2,1,0:T(8,128)(2,1)S(1)} fusion(f32[6,512,2048]{2,1,0:T(8,128)} %get-tuple-element.320, f32[6,512,2048]{2,1,0:T(8,128)} %get-tuple-element.318, f32[6,512]{1,0:T(8,128)S(1)} %get-tuple-element.319, f32[6,512]{1,0:T(8,128)S(1)} %log_add_fusion), kind=kLoop, calls=%fused_computation | loop fusion | flops 25165824 | bytes 62939136 | tf_op jit(solution)/shard_map/convert_element_type | solution.py:279
  341.4 8.3 %fusion.69 = f32[2048,6,64]{0,2,1:T(8,128)S(1)} fusion(f32[2048,6,64]{0,2,1:T(8,128)S(1)} %fusion.77, bf16[512,6,64]{0,2,1:T(8,128)(2,1)} %bitcast.453, f32[6,512,1536]{2,1,0:T(8,128)} %get-tuple-element.316, f32[6,512]{1,0:T(8,128)S(1)} %log_add_fusion.1), kind=kOutput, calls=%fused_computation.127 | convolution fusion | flops 614006784 | bytes 24002560 | tf_op jit(solution)/shard_map/hqk,qhd->khd/dot_general | solution.py:296
  351.6 11.9 %fusion.55 = bf16[2048,6,64]{0,2,1:T(8,128)(2,1)} fusion(f32[2048,6,64]{0,2,1:T(8,128)S(1)} %fusion.69, bf16[512,6,64]{0,2,1:T(8,128)(2,1)S(1)} %bitcast.452, f32[6,512,2048]{2,1,0:T(8,128)} %get-tuple-element.318, f32[6,512]{1,0:T(8,128)} %copy-done.68), kind=kOutput, calls=%fused_computation.109 | convolution fusion | flops 819462144 | bytes 30289920 | tf_op jit(solution)/shard_map/hqk,qhd->khd/dot_general | solution.py:296
  378.4 9.0 %convert_element_type.510 = bf16[2,1024,1152]{1,0,2:T(2,128)(2,1)} reshape(bf16[2048,6,192]{0,2,1:T(8,128)(2,1)} %get-tuple-element.206) | data formatting | bytes 9437184 | tf_op jit(solution)/shard_map/convert_element_type | solution.py:307
  458.0 32.8 %multiply_convert_fusion.3 = (bf16[2048,1536]{1,0:T(8,128)(2,1)S(1)}, f32[2048,1536]{1,0:T(8,128)}, f32[2048,1536]{1,0:T(8,128)}) fusion(f32[1536]{0:T(1024)S(1)} %copy-done.85, bf16[2048,768]{1,0:T(8,128)(2,1)S(1)} %bitcast.462, bf16[768,1536]{1,0:T(8,128)(2,1)S(1)} %bitcast.467), kind=kOutput, calls=%fused_computation.25 | convolution fusion | flops 5039456256 | bytes 36968448 | tf_op jit(solution)/shard_map/dot_general | solution.py:245
  511.1 15.8 %convert_reduce_fusion = (f32[1536]{0:T(1024)S(1)}, bf16[2048,1536]{1,0:T(8,128)(2,1)}) fusion(f32[2048,1536]{1,0:T(8,128)} %get-tuple-element.214, bf16[2048,768]{1,0:T(8,128)(2,1)S(1)} %bitcast.443, bf16[768,1536]{1,0:T(8,128)(2,1)S(1)} %bitcast.470, f32[2048,1536]{1,0:T(8,128)} %get-tuple-element.327, f32[1536]{0:T(1024)S(1)} %copy-done.85), kind=kOutput, calls=%fused_computation.19 | convolution fusion | flops 4885314048 | bytes 36974592 | tf_op jit(solution)/shard_map/dot_general | solution.py:253
  526.9 7.3 %fusion.194 = f32[2,1024,768]{2,1,0:T(8,128)S(1)} fusion(bf16[2,1024,1536]{2,1,0:T(8,128)(2,1)} %bitcast.479, bf16[768,1536,1]{1,0,2:T(8,128)(2,1)S(1)} %bitcast.468), kind=kOutput, calls=%fused_computation.446 | convolution fusion | flops 4831838208 | bytes 14942208 | tf_op jit(solution)/shard_map/gf,df->gd/dot_general | solution.py:258
  538.5 7.0 %fusion.24 = f32[2,2,2,2,48,1536]{5,4,3,2,1,0:T(8,128)} fusion(bf16[2,2,2,2,48,2048]{5,4,3,2,1,0:T(8,128)(2,1)S(1)} %bitcast.459, bf16[2048,1536]{1,0:T(8,128)(2,1)S(1)} %copy-done.87), kind=kOutput, calls=%fused_computation.53 | convolution fusion | flops 4831838208 | bytes 14155776 | tf_op jit(solution)/shard_map/gd,gf->df/dot_general | solution.py:256
  570.8 7.0 %collective-permute-done.46 = bf16[2,2,2,48,1536]{4,3,2,1,0:T(8,128)(2,1)} collective-permute-done((bf16[2,2,2,48,1536]{4,3,2,1,0:T(8,128)(2,1)}, bf16[2,2,2,48,1536]{4,3,2,1,0:T(8,128)(2,1)}, u32[]{:S(2)}, u32[]{:S(2)}) %collective-permute-start.46) | collective-permute-done | bytes 1179680 | tf_op jit(solution)/shard_map/ppermute | solution.py:31
  582.4 15.0 %collective-permute-done.27 = f32[2,2,288]{2,1,0:T(2,128)S(1)} collective-permute-done((f32[2,2,288]{2,1,0:T(2,128)S(1)}, f32[2,2,288]{2,1,0:T(2,128)S(1)}, u32[]{:S(2)}, u32[]{:S(2)}) %collective-permute-start.27) | collective-permute-done | bytes 4640 | tf_op jit(solution)/shard_map/ppermute | solution.py:31
  600.1 6.8 %collective-permute-done.28 = f32[2,288]{1,0:T(2,128)S(1)} collective-permute-done((f32[2,288]{1,0:T(2,128)S(1)}, f32[2,288]{1,0:T(2,128)S(1)}, u32[]{:S(2)}, u32[]{:S(2)}) %collective-permute-start.28) | collective-permute-done | bytes 2336 | tf_op jit(solution)/shard_map/ppermute | solution.py:31
  613.5 30.1 %collective-permute-done.51 = bf16[2,2,48,1536]{3,2,1,0:T(8,128)(2,1)S(1)} collective-permute-done((bf16[2,2,48,1536]{3,2,1,0:T(8,128)(2,1)S(1)}, bf16[2,2,48,1536]{3,2,1,0:T(8,128)(2,1)S(1)}, u32[]{:S(2)}, u32[]{:S(2)}) %collective-permute-start.51) | collective-permute-done | bytes 589856 | tf_op jit(solution)/shard_map/ppermute | solution.py:31
  (534 shorter events, 348.3 us)
Async XLA Ops:
  6.2 19.0 %collective-permute-start.1 = (bf16[1,624]{1,0:T(2,128)(2,1)S(1)}, bf16[1,624]{1,0:T(2,128)(2,1)S(1)}, u32[]{:S(2)}, u32[]{:S(2)}) collective-permute-start(bf16[1,624]{1,0:T(2,128)(2,1)S(1)} %broadcast_in_dim.106), channel_id=1, source_target_pairs={{0,16},{2,18},{4,20},{6,22},{8,24},{10,26},{12,28},{14,30},{16,0},... | collective-permute-start | bytes 3752 | tf_op jit(solution)/shard_map/ppermute | solution.py:31
  11.3 27.7 %collective-permute-start.9 = (bf16[48,384]{1,0:T(8,128)(2,1)S(1)}, bf16[48,384]{1,0:T(8,128)(2,1)S(1)}, u32[]{:S(2)}, u32[]{:S(2)}) collective-permute-start(bf16[48,384]{1,0:T(8,128)(2,1)S(1)} %reshape.1132), channel_id=1, source_target_pairs={{0,4},{2,6},{4,0},{6,2},{8,12},{10,14},{12,8},{14,10},{16,20},{18,... | collective-permute-start | bytes 110600 | tf_op jit(solution)/shard_map/ppermute | solution.py:31
  12.9 33.4 %collective-permute-start.13 = (bf16[48,1536]{1,0:T(8,128)(2,1)}, bf16[48,1536]{1,0:T(8,128)(2,1)S(1)}, u32[]{:S(2)}, u32[]{:S(2)}) collective-permute-start(bf16[48,1536]{1,0:T(8,128)(2,1)} %param.46), channel_id=1, source_target_pairs={{0,16},{2,18},{4,20},{6,22},{8,24},{10,26},{12,28},{14,30},{16,0},... | collective-permute-start | bytes 442376 | tf_op jit(solution)/shard_map/ppermute | solution.py:31
  13.3 33.8 %collective-permute-start.17 = (bf16[48,1536]{1,0:T(8,128)(2,1)}, bf16[48,1536]{1,0:T(8,128)(2,1)S(1)}, u32[]{:S(2)}, u32[]{:S(2)}) collective-permute-start(bf16[48,1536]{1,0:T(8,128)(2,1)} %param.48), channel_id=1, source_target_pairs={{0,2},{2,0},{4,6},{6,4},{8,10},{10,8},{12,14},{14,12},{16,18},{18,... | collective-permute-start | bytes 442376 | tf_op jit(solution)/shard_map/ppermute | solution.py:31
  14.8 86.8 %collective-permute-start = (bf16[1024,768]{1,0:T(8,128)(2,1)}, bf16[1024,768]{1,0:T(8,128)(2,1)}, u32[]{:S(2)}, u32[]{:S(2)}) collective-permute-start(bf16[1024,768]{1,0:T(8,128)(2,1)} %param.35), channel_id=1, source_target_pairs={{0,1},{1,0},{2,3},{3,2},{4,5},{5,4},{6,7},{7,6},{8,9},{9,8},{10,11... | collective-permute-start | bytes 4718600 | tf_op jit(solution)/shard_map/ppermute | solution.py:31
  43.5 61.8 %collective-permute-start.22 = (bf16[1024,768]{1,0:T(8,128)(2,1)}, bf16[1024,768]{1,0:T(8,128)(2,1)S(1)}, u32[]{:S(2)}, u32[]{:S(2)}) collective-permute-start(bf16[1024,768]{1,0:T(8,128)(2,1)} %param.36), channel_id=1, source_target_pairs={{0,1},{1,0},{2,3},{3,2},{4,5},{5,4},{6,7},{7,6},{8,9},{9,8},{10,11... | collective-permute-start | bytes 4718600 | tf_op jit(solution)/shard_map/ppermute | solution.py:31
  54.1 26.1 %collective-permute-start.18 = (bf16[2,48,1536]{2,1,0:T(8,128)(2,1)S(1)}, bf16[2,48,1536]{2,1,0:T(8,128)(2,1)S(1)}, u32[]{:S(2)}, u32[]{:S(2)}) collective-permute-start(bf16[2,48,1536]{2,1,0:T(8,128)(2,1)S(1)} %pad_maximum_fusion.20), channel_id=1, source_target_pairs={{0,16},{2,18},{4,20},{6,22},{8,24},{10,26},{12,28},{14,30},{16,0},... | collective-permute-start | bytes 884744 | tf_op jit(solution)/shard_map/ppermute | solution.py:31
  54.2 27.6 %collective-permute-start.12 = (bf16[2,2,2,48,384]{4,3,2,1,0:T(8,128)(2,1)S(1)}, bf16[2,2,2,48,384]{4,3,2,1,0:T(8,128)(2,1)S(1)}, u32[]{:S(2)}, u32[]{:S(2)}) collective-permute-start(bf16[2,2,2,48,384]{4,3,2,1,0:T(8,128)(2,1)S(1)} %pad_maximum_fusion.18), channel_id=1, source_target_pairs={{0,8},{2,10},{4,12},{6,14},{8,0},{10,2},{12,4},{14,6},{16,24},{18,... | collective-permute-start | bytes 884744 | tf_op jit(solution)/shard_map/ppermute | solution.py:31
  59.5 29.5 %collective-permute-start.7 = (bf16[2,2,48,1152]{3,2,1,0:T(8,128)(2,1)S(1)}, bf16[2,2,48,1152]{3,2,1,0:T(8,128)(2,1)S(1)}, u32[]{:S(2)}, u32[]{:S(2)}) collective-permute-start(bf16[2,2,48,1152]{3,2,1,0:T(8,128)(2,1)S(1)} %pad_maximum_fusion.15), channel_id=1, source_target_pairs={{0,16},{2,18},{4,20},{6,22},{8,24},{10,26},{12,28},{14,30},{16,0},... | collective-permute-start | bytes 1327112 | tf_op jit(solution)/shard_map/ppermute | solution.py:31
  81.8 16.8 %collective-permute-start.19 = (bf16[2,2,48,1536]{3,2,1,0:T(8,128)(2,1)S(1)}, bf16[2,2,48,1536]{3,2,1,0:T(8,128)(2,1)S(1)}, u32[]{:S(2)}, u32[]{:S(2)}) collective-permute-start(bf16[2,2,48,1536]{3,2,1,0:T(8,128)(2,1)S(1)} %pad_maximum_fusion.14), channel_id=1, source_target_pairs={{0,8},{2,10},{4,12},{6,14},{8,0},{10,2},{12,4},{14,6},{16,24},{18,... | collective-permute-start | bytes 1769480 | tf_op jit(solution)/shard_map/ppermute | solution.py:31
  90.3 36.0 %collective-permute-start.8 = (bf16[2,2,2,48,1152]{4,3,2,1,0:T(8,128)(2,1)}, bf16[2,2,2,48,1152]{4,3,2,1,0:T(8,128)(2,1)}, u32[]{:S(2)}, u32[]{:S(2)}) collective-permute-start(bf16[2,2,2,48,1152]{4,3,2,1,0:T(8,128)(2,1)} %pad_maximum_fusion.11), channel_id=1, source_target_pairs={{0,8},{2,10},{4,12},{6,14},{8,0},{10,2},{12,4},{14,6},{16,24},{18,... | collective-permute-start | bytes 2654216 | tf_op jit(solution)/shard_map/ppermute | solution.py:31
  92.2 362.3 %collective-permute-start.16 = (bf16[2,2,2,48,1536]{4,3,2,1,0:T(8,128)(2,1)}, bf16[2,2,2,48,1536]{4,3,2,1,0:T(8,128)(2,1)}, u32[]{:S(2)}, u32[]{:S(2)}) collective-permute-start(bf16[2,2,2,48,1536]{4,3,2,1,0:T(8,128)(2,1)} %pad_maximum_fusion.7), channel_id=1, source_target_pairs={{0,2},{2,0},{4,6},{6,4},{8,10},{10,8},{12,14},{14,12},{16,18},{18,... | collective-permute-start | bytes 3538952 | tf_op jit(solution)/shard_map/ppermute | solution.py:31
  100.0 397.7 %collective-permute-start.20 = (bf16[2,2,2,48,1536]{4,3,2,0,1:T(8,128)(2,1)}, bf16[2,2,2,48,1536]{4,3,2,0,1:T(8,128)(2,1)}, u32[]{:S(2)}, u32[]{:S(2)}) collective-permute-start(bf16[2,2,2,48,1536]{4,3,2,0,1:T(8,128)(2,1)} %pad_maximum_fusion.8), channel_id=1, source_target_pairs={{0,4},{2,6},{4,0},{6,2},{8,12},{10,14},{12,8},{14,10},{16,20},{18,... | collective-permute-start | bytes 3538952 | tf_op jit(solution)/shard_map/ppermute | solution.py:31
  370.7 40.0 %collective-permute-start.42 = (bf16[2,2,2,48,384]{4,3,2,1,0:T(8,128)(2,1)}, bf16[2,2,2,48,384]{4,3,2,1,0:T(8,128)(2,1)}, u32[]{:S(2)}, u32[]{:S(2)}) collective-permute-start(bf16[2,2,2,48,384]{4,3,2,1,0:T(8,128)(2,1)} %fusion.120), channel_id=1, source_target_pairs={{0,8},{2,10},{4,12},{6,14},{8,0},{10,2},{12,4},{14,6},{16,24},{18,... | collective-permute-start | bytes 884744 | tf_op jit(solution)/shard_map/ppermute | solution.py:31
  395.8 16.7 %collective-permute-start.34 = (bf16[2,2,2,48,384]{4,3,2,0,1:T(8,128)(2,1)}, bf16[2,2,2,48,384]{4,3,2,0,1:T(8,128)(2,1)}, u32[]{:S(2)}, u32[]{:S(2)}) collective-permute-start(bf16[2,2,2,48,384]{4,3,2,0,1:T(8,128)(2,1)} %fusion.124), channel_id=1, source_target_pairs={{0,4},{2,6},{4,0},{6,2},{8,12},{10,14},{12,8},{14,10},{16,20},{18,... | collective-permute-start | bytes 884744 | tf_op jit(solution)/shard_map/ppermute | solution.py:31
  412.4 137.7 %collective-permute-start.24 = (bf16[1024,768]{1,0:T(8,128)(2,1)}, bf16[1024,768]{1,0:T(8,128)(2,1)}, u32[]{:S(2)}, u32[]{:S(2)}) collective-permute-start(bf16[1024,768]{1,0:T(8,128)(2,1)} %fusion.74), channel_id=1, source_target_pairs={{0,1},{1,0},{2,3},{3,2},{4,5},{5,4},{6,7},{7,6},{8,9},{9,8},{10,11... | collective-permute-start | bytes 4718600 | tf_op jit(solution)/shard_map/ppermute | solution.py:31
  511.1 43.9 %collective-permute-start.21 = (bf16[1024,768]{1,0:T(8,128)(2,1)}, bf16[1024,768]{1,0:T(8,128)(2,1)}, u32[]{:S(2)}, u32[]{:S(2)}) collective-permute-start(bf16[1024,768]{1,0:T(8,128)(2,1)} %fusion.72), channel_id=1, source_target_pairs={{0,1},{1,0},{2,3},{3,2},{4,5},{5,4},{6,7},{7,6},{8,9},{9,8},{10,11... | collective-permute-start | bytes 4718600 | tf_op jit(solution)/shard_map/ppermute | solution.py:31
  535.6 14.6 %collective-permute-start.23 = (bf16[1024,768]{1,0:T(8,128)(2,1)}, bf16[1024,768]{1,0:T(8,128)(2,1)S(1)}, u32[]{:S(2)}, u32[]{:S(2)}) collective-permute-start(bf16[1024,768]{1,0:T(8,128)(2,1)} %fusion.73), channel_id=1, source_target_pairs={{0,1},{1,0},{2,3},{3,2},{4,5},{5,4},{6,7},{7,6},{8,9},{9,8},{10,11... | collective-permute-start | bytes 4718600 | tf_op jit(solution)/shard_map/ppermute | solution.py:31
  548.9 28.9 %collective-permute-start.46 = (bf16[2,2,2,48,1536]{4,3,2,1,0:T(8,128)(2,1)}, bf16[2,2,2,48,1536]{4,3,2,1,0:T(8,128)(2,1)}, u32[]{:S(2)}, u32[]{:S(2)}) collective-permute-start(bf16[2,2,2,48,1536]{4,3,2,1,0:T(8,128)(2,1)} %fusion.99), channel_id=1, source_target_pairs={{0,4},{2,6},{4,0},{6,2},{8,12},{10,14},{12,8},{14,10},{16,20},{18,... | collective-permute-start | bytes 3538952 | tf_op jit(solution)/shard_map/ppermute | solution.py:31
  568.4 29.7 %collective-permute-start.50 = (bf16[2,2,2,48,1536]{4,3,2,1,0:T(8,128)(2,1)S(1)}, bf16[2,2,2,48,1536]{4,3,2,1,0:T(8,128)(2,1)S(1)}, u32[]{:S(2)}, u32[]{:S(2)}) collective-permute-start(bf16[2,2,2,48,1536]{4,3,2,1,0:T(8,128)(2,1)S(1)} %fusion.100), channel_id=1, source_target_pairs={{0,8},{2,10},{4,12},{6,14},{8,0},{10,2},{12,4},{14,6},{16,24},{18,... | collective-permute-start | bytes 3538952 | tf_op jit(solution)/shard_map/ppermute | solution.py:31
  580.2 17.2 %collective-permute-start.27 = (f32[2,2,288]{2,1,0:T(2,128)S(1)}, f32[2,2,288]{2,1,0:T(2,128)S(1)}, u32[]{:S(2)}, u32[]{:S(2)}) collective-permute-start(f32[2,2,288]{2,1,0:T(2,128)S(1)} %fusion.149), channel_id=1, source_target_pairs={{0,8},{2,10},{4,12},{6,14},{8,0},{10,2},{12,4},{14,6},{16,24},{18,... | collective-permute-start | bytes 13832 | tf_op jit(solution)/shard_map/ppermute | solution.py:31
  580.4 31.9 %collective-permute-start.47 = (bf16[2,2,48,1536]{3,2,1,0:T(8,128)(2,1)S(1)}, bf16[2,2,48,1536]{3,2,1,0:T(8,128)(2,1)S(1)}, u32[]{:S(2)}, u32[]{:S(2)}) collective-permute-start(bf16[2,2,48,1536]{3,2,1,0:T(8,128)(2,1)S(1)} %fusion.112), channel_id=1, source_target_pairs={{0,8},{2,10},{4,12},{6,14},{8,0},{10,2},{12,4},{14,6},{16,24},{18,... | collective-permute-start | bytes 1769480 | tf_op jit(solution)/shard_map/ppermute | solution.py:31
  607.1 36.6 %collective-permute-start.51 = (bf16[2,2,48,1536]{3,2,1,0:T(8,128)(2,1)S(1)}, bf16[2,2,48,1536]{3,2,1,0:T(8,128)(2,1)S(1)}, u32[]{:S(2)}, u32[]{:S(2)}) collective-permute-start(bf16[2,2,48,1536]{3,2,1,0:T(8,128)(2,1)S(1)} %fusion.113), channel_id=1, source_target_pairs={{0,16},{2,18},{4,20},{6,22},{8,24},{10,26},{12,28},{14,30},{16,0},... | collective-permute-start | bytes 1769480 | tf_op jit(solution)/shard_map/ppermute | solution.py:31
  612.5 37.3 %collective-permute-start.48 = (bf16[2,48,1536]{2,1,0:T(8,128)(2,1)S(1)}, bf16[2,48,1536]{2,1,0:T(8,128)(2,1)S(1)}, u32[]{:S(2)}, u32[]{:S(2)}) collective-permute-start(bf16[2,48,1536]{2,1,0:T(8,128)(2,1)S(1)} %fusion.121), channel_id=1, source_target_pairs={{0,16},{2,18},{4,20},{6,22},{8,24},{10,26},{12,28},{14,30},{16,0},... | collective-permute-start | bytes 884744 | tf_op jit(solution)/shard_map/ppermute | solution.py:31
  (125 other events, 1318.0 us)

commit v3 on v2

--- a/solution.py
+++ b/solution.py
@@ -264,6 +264,7 @@
     grad_dense = jnp.einsum(
         "gd,gc->dc", cot_all, heads_flat, preferred_element_type=jnp.float32
     )
+    grad_heads, grad_fc, grad_proj = lax.optimization_barrier((grad_heads, grad_fc, grad_proj))
     query_grads = []
     grad_key = jnp.zeros((group_rows, head_count, head_dim), jnp.float32)
     grad_value = jnp.zeros((group_rows, head_count, head_dim), jnp.float32)

time: 667 us -> 678 us (1.016)
  local copies, waits for them, and re-layouts: 81.6 us -> 67.4 us
  matrix products: 245 us -> 259 us
  waiting for transfers between devices: 147 us -> 157 us
    ppermute x54, waiting for transfers between devices: 147 us -> 157 us  [exchange(): return lax.ppermute(values, axis, [(i, i ^ step) for i in range(size)])]
    unnamed x191 -> x231, local copies, waits for them, and re-layouts: 26 us -> 17.1 us
  transfers between devices with their start and end apart: 54 -> 54, of which waited for: 28 -> 31; matrix products, arithmetic and copies ran while one was open for 65% -> 40% of each run, Pallas kernels for 0% -> 0%
where the time goes in v3:
time: 678 us; the launch traced here: 670 us
  matrix products  259 us (38%)
  waiting for transfers between devices  157 us (23%)
  other arithmetic  130 us (19%)
  local copies, waits for them, and re-layouts  67.4 us (10%)
  starting transfers between devices  53.6 us (8%)
    ppermute x54, waiting for transfers between devices, exchange(): return lax.ppermute(values, axis, [(i, i ^ step) for i in range(size)])  157 us
    ppermute x54, starting transfers between devices, exchange(): return lax.ppermute(values, axis, [(i, i ^ step) for i in range(size)])  53.6 us
    dot_general x4, matrix products, body(): jnp.einsum('qhd,khd->hqk', heads_blk, value_low[:end_row], preferred_elem...  42.4 us
    convert_element_type x4, other arithmetic, body(): grad_scores = (probs * (grad_probs - row_delta)).astype(jnp.bfloat16)  40.5 us
    dot_general x1, matrix products, body(): jnp.dot(normed_mlp, w_fc, preferred_element_type=jnp.float32) + my_bias_fc  32.7 us
    dot_general x4, matrix products, body(): jnp.einsum('hqk,khd->qhd', prob_low, value_low[:end_row], preferred_eleme...  27.1 us
    dot_general x4, matrix products, masked_scores(): jnp.einsum('qhd,khd->hqk', query_low[begin_row:end_row], key_low[:end_row...  25.5 us
    dot_general x4, matrix products, body(): jnp.einsum('hqk,qhd->khd', probs.astype(jnp.bfloat16), heads_blk, preferr...  24.8 us
  transfers between devices with their start and end apart: 54, of which 31 were waited for; matrix products, arithmetic and copies ran while one was open for 40% of the time, Pallas kernels for 0%

profile of v3, /device:TPU:0, one launch (start us, length us, event | category | flops | bytes accessed | tf_op | source)
XLA Modules:
  0.0 669.9 jit_solution(3922018362787859079)
XLA Ops:
  58.9 20.6 %collective-permute-done.18 = bf16[2,48,1536]{2,1,0:T(8,128)(2,1)S(1)} collective-permute-done((bf16[2,48,1536]{2,1,0:T(8,128)(2,1)S(1)}, bf16[2,48,1536]{2,1,0:T(8,128)(2,1)S(1)}, u32[]{:S(2)}, u32[]{:S(2)}) %collective-permute-start.18) | collective-permute-done | bytes 294944 | tf_op jit(solution)/shard_map/ppermute | solution.py:31
  152.6 10.0 %fusion.194 = (f32[6,512]{1,0:T(8,128)}, f32[6,512,1536]{2,1,0:T(8,128)}) fusion(bf16[2048,6,48]{0,2,1:T(8,128)(2,1)S(1)} %get-tuple-element.227, bf16[2048,6,16]{0,2,1:T(8,128)(2,1)S(1)} %get-tuple-element.221, bf16[2048,6,48]{0,2,1:T(8,128)(2,1)S(1)} %get-tuple-element.228, bf16[2048,6,16]{0,2,1:T(8,128)(2,1)S(1)} %get-tuple-element.222, ...), kind=kOutput, calls=%fused_computation.450 | convolution fusion | flops 621278208 | bytes 22818816 | tf_op jit(solution)/shard_map/qhd,khd->hqk/dot_general | solution.py:208
  162.6 9.0 %fusion.2 = f32[6,512]{1,0:T(8,128)S(1)} fusion(f32[6,512,1536]{2,1,0:T(8,128)} %get-tuple-element.319, f32[6,512]{1,0:T(8,128)} %get-tuple-element.318), kind=kLoop, calls=%fused_computation.15 | loop fusion | flops 9434112 | bytes 18898944 | tf_op jit(solution)/shard_map/reduce_sum | solution.py:228
  171.7 9.4 %fusion.90 = bf16[6,64,512]{2,1,0:T(8,128)(2,1)} fusion(f32[6,512,1536]{2,1,0:T(8,128)} %get-tuple-element.319, f32[6,512]{1,0:T(8,128)S(1)} %fusion.2, f32[6,512]{1,0:T(8,128)S(1)} %copy-done.85, bf16[2048,6,192]{0,2,1:T(8,128)(2,1)} %copy-done.10), kind=kOutput, calls=%fused_computation.174 | convolution fusion | flops 618332160 | bytes 20471808 | tf_op jit(solution)/shard_map/hqk,khd->qhd/dot_general | solution.py:232
  183.0 10.6 %fusion.195 = (f32[6,512]{1,0:T(8,128)S(1)}, f32[6,512,2048]{2,1,0:T(8,128)}) fusion(bf16[512,6,64]{0,2,1:T(8,128)(2,1)S(1)} %copy-done.56, bf16[2048,6,16]{0,2,1:T(8,128)(2,1)S(1)} %get-tuple-element.221, bf16[2048,6,48]{0,2,1:T(8,128)(2,1)S(1)} %get-tuple-element.227, pred[512,2048]{1,0:T(8,128)(4,1)S(1)} %copy-done.62), kind=kOutput, calls=%fused_computation.451 | convolution fusion | flops 827323392 | bytes 28192768 | tf_op jit(solution)/shard_map/qhd,khd->hqk/dot_general | solution.py:208
  193.6 10.4 %fusion = f32[6,512]{1,0:T(8,128)S(1)} fusion(f32[6,512,2048]{2,1,0:T(8,128)} %get-tuple-element.321, f32[6,512]{1,0:T(8,128)S(1)} %get-tuple-element.320), kind=kLoop, calls=%fused_computation.6 | loop fusion | flops 12579840 | bytes 25190400 | tf_op jit(solution)/shard_map/reduce_sum | solution.py:228
  204.1 11.2 %fusion.91 = bf16[6,64,512]{2,1,0:T(8,128)(2,1)S(1)} fusion(f32[6,512,2048]{2,1,0:T(8,128)} %get-tuple-element.321, f32[6,512]{1,0:T(8,128)S(1)} %fusion, f32[6,512]{1,0:T(8,128)S(1)} %get-tuple-element.320, bf16[2048,6,192]{0,2,1:T(8,128)(2,1)} %copy-done.10), kind=kOutput, calls=%fused_computation.175 | convolution fusion | flops 824377344 | bytes 27156480 | tf_op jit(solution)/shard_map/hqk,khd->qhd/dot_general | solution.py:232
  249.7 32.7 %multiply_convert_fusion.3 = (bf16[2048,1536]{1,0:T(8,128)(2,1)S(1)}, f32[2048,1536]{1,0:T(8,128)}, f32[2048,1536]{1,0:T(8,128)}) fusion(f32[1536]{0:T(1024)S(1)} %copy-done.99, bf16[2048,768]{1,0:T(8,128)(2,1)S(1)} %bitcast.449, bf16[768,1536]{1,0:T(8,128)(2,1)S(1)} %bitcast.456), kind=kOutput, calls=%fused_computation.25 | convolution fusion | flops 5039456256 | bytes 36968448 | tf_op jit(solution)/shard_map/dot_general | solution.py:245
  282.4 6.8 %fusion.199 = f32[768,1536]{1,0:T(8,128)} fusion(bf16[2048,768]{1,0:T(8,128)(2,1)S(1)} %bitcast.428, bf16[2048,1536]{1,0:T(8,128)(2,1)S(1)} %get-tuple-element.219), kind=kOutput, calls=%fused_computation.455 | convolution fusion | flops 4831838208 | bytes 14155776 | tf_op jit(solution)/shard_map/gd,gf->df/dot_general | solution.py:254
  290.9 7.2 %fusion.196 = f32[2048,768]{1,0:T(8,128)} fusion(bf16[2048,1536]{1,0:T(8,128)(2,1)S(1)} %get-tuple-element.219, bf16[768,1536]{1,0:T(8,128)(2,1)S(1)} %bitcast.458), kind=kOutput, calls=%fused_computation.452 | convolution fusion | flops 4831838208 | bytes 14942208 | tf_op jit(solution)/shard_map/gf,df->gd/dot_general | solution.py:248
  298.1 16.6 %convert_reduce_fusion = (f32[1536]{0:T(1024)}, bf16[2048,1536]{1,0:T(8,128)(2,1)}) fusion(f32[2048,1536]{1,0:T(8,128)} %get-tuple-element.220, bf16[2048,768]{1,0:T(8,128)(2,1)S(1)} %bitcast.429, bf16[768,1536]{1,0:T(8,128)(2,1)} %bitcast.459, f32[2048,1536]{1,0:T(8,128)} %get-tuple-element.315, f32[1536]{0:T(1024)S(1)} %copy-done.99), kind=kOutput, calls=%fused_computation.19 | convolution fusion | flops 4885314048 | bytes 36974592 | tf_op jit(solution)/shard_map/dot_general | solution.py:253
  314.7 9.7 %fusion.198 = f32[768,1536]{1,0:T(8,128)} fusion(bf16[2048,768]{1,0:T(8,128)(2,1)} %fusion.25, bf16[2048,1536]{1,0:T(8,128)(2,1)} %get-tuple-element.331), kind=kOutput, calls=%fused_computation.454 | convolution fusion | flops 4831838208 | bytes 14155776 | tf_op jit(solution)/shard_map/gd,gf->df/dot_general | solution.py:256
  341.0 7.8 %multiply_reduce_fusion.2 = (f32[6,512]{1,0:T(8,128)S(1)}, f32[6,512,1024]{2,1,0:T(8,128)}) fusion(f32[6,512,1024]{2,1,0:T(8,128)S(1)} %bitcast.413, f32[6,512]{1,0:T(8,128)S(1)} %copy-done.67, bf16[2048,6,192]{0,2,1:T(8,128)(2,1)} %copy-done.10, bf16[2048,6,64]{0,2,1:T(8,128)(2,1)S(1)} %bitcast.435), kind=kOutput, calls=%fused_computation.22 | convolution fusion | flops 412087296 | bytes 26374144 | tf_op jit(solution)/shard_map/qhd,khd->hqk/dot_general | solution.py:276
  364.0 12.5 %multiply_reduce_fusion.1 = (f32[6,512]{1,0:T(8,128)S(1)}, f32[6,512,1536]{2,1,0:T(8,128)}) fusion(f32[6,512,1536]{2,1,0:T(8,128)} %get-tuple-element.319, f32[6,512]{1,0:T(8,128)S(1)} %copy-done.63, bf16[2048,6,192]{0,2,1:T(8,128)(2,1)} %copy-done.10, bf16[2048,6,64]{0,2,1:T(8,128)(2,1)S(1)} %bitcast.436), kind=kOutput, calls=%fused_computation.10 | convolution fusion | flops 618132480 | bytes 39350272 | tf_op jit(solution)/shard_map/qhd,khd->hqk/dot_general | solution.py:276
  376.5 12.9 %multiply_convert_fusion.1 = bf16[6,512,1536]{2,1,0:T(8,128)(2,1)S(1)} fusion(f32[6,512,1536]{2,1,0:T(8,128)} %get-tuple-element.325, f32[6,512,1536]{2,1,0:T(8,128)} %get-tuple-element.319, f32[6,512]{1,0:T(8,128)S(1)} %get-tuple-element.324, f32[6,512]{1,0:T(8,128)S(1)} %copy-done.63), kind=kLoop, calls=%fused_computation.9 | loop fusion | flops 18874368 | bytes 47210496 | tf_op jit(solution)/shard_map/convert_element_type | solution.py:280
  398.3 16.5 %multiply_reduce_fusion = (f32[6,512]{1,0:T(8,128)S(1)}, f32[6,512,2048]{2,1,0:T(8,128)}) fusion(f32[6,512,2048]{2,1,0:T(8,128)} %get-tuple-element.321, f32[6,512]{1,0:T(8,128)S(1)} %copy-done.64, bf16[2048,6,192]{0,2,1:T(8,128)(2,1)} %copy-done.10, bf16[2048,6,64]{0,2,1:T(8,128)(2,1)} %bitcast.432), kind=kOutput, calls=%fused_computation.1 | convolution fusion | flops 824177664 | bytes 52322304 | tf_op jit(solution)/shard_map/qhd,khd->hqk/dot_general | solution.py:276
  414.8 16.6 %multiply_convert_fusion = bf16[6,512,2048]{2,1,0:T(8,128)(2,1)S(1)} fusion(f32[6,512,2048]{2,1,0:T(8,128)} %get-tuple-element.323, f32[6,512,2048]{2,1,0:T(8,128)} %get-tuple-element.321, f32[6,512]{1,0:T(8,128)S(1)} %get-tuple-element.322, f32[6,512]{1,0:T(8,128)S(1)} %copy-done.65), kind=kLoop, calls=%fused_computation | loop fusion | flops 25165824 | bytes 62939136 | tf_op jit(solution)/shard_map/convert_element_type | solution.py:280
  463.5 8.3 %fusion.65 = f32[2048,6,64]{0,2,1:T(8,128)S(1)} fusion(f32[2048,6,64]{0,2,1:T(8,128)S(1)} %fusion.73, f32[6,512,1536]{2,1,0:T(8,128)} %get-tuple-element.319, f32[6,512]{1,0:T(8,128)S(1)} %copy-done.63, bf16[2048,6,64]{0,2,1:T(8,128)(2,1)S(1)} %bitcast.438), kind=kOutput, calls=%fused_computation.123 | convolution fusion | flops 614006784 | bytes 24002560 | tf_op jit(solution)/shard_map/hqk,qhd->khd/dot_general | solution.py:297
  471.8 11.8 %fusion.51 = bf16[2048,6,64]{0,2,1:T(8,128)(2,1)} fusion(f32[2048,6,64]{0,2,1:T(8,128)S(1)} %fusion.65, f32[6,512,2048]{2,1,0:T(8,128)} %get-tuple-element.321, f32[6,512]{1,0:T(8,128)S(1)} %copy-done.66, bf16[2048,6,64]{0,2,1:T(8,128)(2,1)S(1)} %bitcast.439), kind=kOutput, calls=%fused_computation.105 | convolution fusion | flops 819462144 | bytes 30294016 | tf_op jit(solution)/shard_map/hqk,qhd->khd/dot_general | solution.py:297
  483.7 7.9 %fusion.197 = f32[2,1024,768]{2,1,0:T(8,128)S(1)} fusion(bf16[2,1024,1536]{2,1,0:T(8,128)(2,1)} %bitcast.468, bf16[768,1536,1]{1,0,2:T(8,128)(2,1)} %bitcast.457), kind=kOutput, calls=%fused_computation.453 | convolution fusion | flops 4831838208 | bytes 14942208 | tf_op jit(solution)/shard_map/gf,df->gd/dot_general | solution.py:258
  502.6 9.3 %convert_element_type.513 = bf16[2,1024,1152]{1,0,2:T(2,128)(2,1)} reshape(bf16[2048,6,192]{0,2,1:T(8,128)(2,1)} %get-tuple-element.212) | data formatting | bytes 9437184 | tf_op jit(solution)/shard_map/convert_element_type | solution.py:308
  529.9 8.6 %collective-permute-done.38 = bf16[2,2,2,48,384]{4,3,1,2,0:T(8,128)(2,1)S(1)} collective-permute-done((bf16[2,2,2,48,384]{4,3,1,2,0:T(8,128)(2,1)S(1)}, bf16[2,2,2,48,384]{4,3,1,2,0:T(8,128)(2,1)S(1)}, u32[]{:S(2)}, u32[]{:S(2)}) %collective-permute-start.38) | collective-permute-done | bytes 294944 | tf_op jit(solution)/shard_map/ppermute | solution.py:31
  550.3 7.3 %collective-permute-done.39 = bf16[2,2,48,384]{3,2,0,1:T(8,128)(2,1)S(1)} collective-permute-done((bf16[2,2,48,384]{3,2,0,1:T(8,128)(2,1)S(1)}, bf16[2,2,48,384]{3,2,0,1:T(8,128)(2,1)S(1)}, u32[]{:S(2)}, u32[]{:S(2)}) %collective-permute-start.39) | collective-permute-done | bytes 147488 | tf_op jit(solution)/shard_map/ppermute | solution.py:31
  624.1 30.1 %collective-permute-done.51 = bf16[2,2,48,1536]{3,2,0,1:T(8,128)(2,1)S(1)} collective-permute-done((bf16[2,2,48,1536]{3,2,0,1:T(8,128)(2,1)S(1)}, bf16[2,2,48,1536]{3,2,0,1:T(8,128)(2,1)S(1)}, u32[]{:S(2)}, u32[]{:S(2)}) %collective-permute-start.51) | collective-permute-done | bytes 589856 | tf_op jit(solution)/shard_map/ppermute | solution.py:31
  (575 shorter events, 362.8 us)
Async XLA Ops:
  6.2 18.2 %collective-permute-start.1 = (bf16[1,624]{1,0:T(2,128)(2,1)S(1)}, bf16[1,624]{1,0:T(2,128)(2,1)S(1)}, u32[]{:S(2)}, u32[]{:S(2)}) collective-permute-start(bf16[1,624]{1,0:T(2,128)(2,1)S(1)} %broadcast_in_dim.106), channel_id=1, source_target_pairs={{0,16},{2,18},{4,20},{6,22},{8,24},{10,26},{12,28},{14,30},{16,0},... | collective-permute-start | bytes 3752 | tf_op jit(solution)/shard_map/ppermute | solution.py:31
  11.3 27.0 %collective-permute-start.9 = (bf16[48,384]{1,0:T(8,128)(2,1)S(1)}, bf16[48,384]{1,0:T(8,128)(2,1)S(1)}, u32[]{:S(2)}, u32[]{:S(2)}) collective-permute-start(bf16[48,384]{1,0:T(8,128)(2,1)S(1)} %reshape.1132), channel_id=1, source_target_pairs={{0,4},{2,6},{4,0},{6,2},{8,12},{10,14},{12,8},{14,10},{16,20},{18,... | collective-permute-start | bytes 110600 | tf_op jit(solution)/shard_map/ppermute | solution.py:31
  12.9 32.7 %collective-permute-start.13 = (bf16[48,1536]{1,0:T(8,128)(2,1)}, bf16[48,1536]{1,0:T(8,128)(2,1)S(1)}, u32[]{:S(2)}, u32[]{:S(2)}) collective-permute-start(bf16[48,1536]{1,0:T(8,128)(2,1)} %param.46), channel_id=1, source_target_pairs={{0,16},{2,18},{4,20},{6,22},{8,24},{10,26},{12,28},{14,30},{16,0},... | collective-permute-start | bytes 442376 | tf_op jit(solution)/shard_map/ppermute | solution.py:31
  13.3 33.0 %collective-permute-start.17 = (bf16[48,1536]{1,0:T(8,128)(2,1)}, bf16[48,1536]{1,0:T(8,128)(2,1)S(1)}, u32[]{:S(2)}, u32[]{:S(2)}) collective-permute-start(bf16[48,1536]{1,0:T(8,128)(2,1)} %param.48), channel_id=1, source_target_pairs={{0,2},{2,0},{4,6},{6,4},{8,10},{10,8},{12,14},{14,12},{16,18},{18,... | collective-permute-start | bytes 442376 | tf_op jit(solution)/shard_map/ppermute | solution.py:31
  14.8 86.0 %collective-permute-start = (bf16[1024,768]{1,0:T(8,128)(2,1)}, bf16[1024,768]{1,0:T(8,128)(2,1)}, u32[]{:S(2)}, u32[]{:S(2)}) collective-permute-start(bf16[1024,768]{1,0:T(8,128)(2,1)} %param.35), channel_id=1, source_target_pairs={{0,1},{1,0},{2,3},{3,2},{4,5},{5,4},{6,7},{7,6},{8,9},{9,8},{10,11... | collective-permute-start | bytes 4718600 | tf_op jit(solution)/shard_map/ppermute | solution.py:31
  42.8 65.2 %collective-permute-start.22 = (bf16[1024,768]{1,0:T(8,128)(2,1)}, bf16[1024,768]{1,0:T(8,128)(2,1)S(1)}, u32[]{:S(2)}, u32[]{:S(2)}) collective-permute-start(bf16[1024,768]{1,0:T(8,128)(2,1)} %param.36), channel_id=1, source_target_pairs={{0,1},{1,0},{2,3},{3,2},{4,5},{5,4},{6,7},{7,6},{8,9},{9,8},{10,11... | collective-permute-start | bytes 4718600 | tf_op jit(solution)/shard_map/ppermute | solution.py:31
  42.9 10.5 %collective-permute-start.11 = (bf16[2,2,48,384]{3,2,1,0:T(8,128)(2,1)S(1)}, bf16[2,2,48,384]{3,2,1,0:T(8,128)(2,1)S(1)}, u32[]{:S(2)}, u32[]{:S(2)}) collective-permute-start(bf16[2,2,48,384]{3,2,1,0:T(8,128)(2,1)S(1)} %pad_maximum_fusion.25), channel_id=1, source_target_pairs={{0,16},{2,18},{4,20},{6,22},{8,24},{10,26},{12,28},{14,30},{16,0},... | collective-permute-start | bytes 442376 | tf_op jit(solution)/shard_map/ppermute | solution.py:31
  46.3 12.5 %collective-permute-start.14 = (bf16[2,48,1536]{2,1,0:T(8,128)(2,1)S(1)}, bf16[2,48,1536]{2,1,0:T(8,128)(2,1)S(1)}, u32[]{:S(2)}, u32[]{:S(2)}) collective-permute-start(bf16[2,48,1536]{2,1,0:T(8,128)(2,1)S(1)} %pad_maximum_fusion.19), channel_id=1, source_target_pairs={{0,8},{2,10},{4,12},{6,14},{8,0},{10,2},{12,4},{14,6},{16,24},{18,... | collective-permute-start | bytes 884744 | tf_op jit(solution)/shard_map/ppermute | solution.py:31
  53.4 26.1 %collective-permute-start.18 = (bf16[2,48,1536]{2,1,0:T(8,128)(2,1)S(1)}, bf16[2,48,1536]{2,1,0:T(8,128)(2,1)S(1)}, u32[]{:S(2)}, u32[]{:S(2)}) collective-permute-start(bf16[2,48,1536]{2,1,0:T(8,128)(2,1)S(1)} %pad_maximum_fusion.20), channel_id=1, source_target_pairs={{0,16},{2,18},{4,20},{6,22},{8,24},{10,26},{12,28},{14,30},{16,0},... | collective-permute-start | bytes 884744 | tf_op jit(solution)/shard_map/ppermute | solution.py:31
  53.5 27.6 %collective-permute-start.12 = (bf16[2,2,2,48,384]{4,3,2,1,0:T(8,128)(2,1)S(1)}, bf16[2,2,2,48,384]{4,3,2,1,0:T(8,128)(2,1)S(1)}, u32[]{:S(2)}, u32[]{:S(2)}) collective-permute-start(bf16[2,2,2,48,384]{4,3,2,1,0:T(8,128)(2,1)S(1)} %pad_maximum_fusion.18), channel_id=1, source_target_pairs={{0,8},{2,10},{4,12},{6,14},{8,0},{10,2},{12,4},{14,6},{16,24},{18,... | collective-permute-start | bytes 884744 | tf_op jit(solution)/shard_map/ppermute | solution.py:31
  58.8 29.5 %collective-permute-start.7 = (bf16[2,2,48,1152]{3,2,1,0:T(8,128)(2,1)S(1)}, bf16[2,2,48,1152]{3,2,1,0:T(8,128)(2,1)S(1)}, u32[]{:S(2)}, u32[]{:S(2)}) collective-permute-start(bf16[2,2,48,1152]{3,2,1,0:T(8,128)(2,1)S(1)} %pad_maximum_fusion.15), channel_id=1, source_target_pairs={{0,16},{2,18},{4,20},{6,22},{8,24},{10,26},{12,28},{14,30},{16,0},... | collective-permute-start | bytes 1327112 | tf_op jit(solution)/shard_map/ppermute | solution.py:31
  79.5 10.5 %collective-permute-start.15 = (bf16[2,2,48,1536]{3,2,1,0:T(8,128)(2,1)S(1)}, bf16[2,2,48,1536]{3,2,1,0:T(8,128)(2,1)S(1)}, u32[]{:S(2)}, u32[]{:S(2)}) collective-permute-start(bf16[2,2,48,1536]{3,2,1,0:T(8,128)(2,1)S(1)} %pad_maximum_fusion.13), channel_id=1, source_target_pairs={{0,4},{2,6},{4,0},{6,2},{8,12},{10,14},{12,8},{14,10},{16,20},{18,... | collective-permute-start | bytes 1769480 | tf_op jit(solution)/shard_map/ppermute | solution.py:31
  81.1 16.8 %collective-permute-start.19 = (bf16[2,2,48,1536]{3,2,1,0:T(8,128)(2,1)S(1)}, bf16[2,2,48,1536]{3,2,1,0:T(8,128)(2,1)S(1)}, u32[]{:S(2)}, u32[]{:S(2)}) collective-permute-start(bf16[2,2,48,1536]{3,2,1,0:T(8,128)(2,1)S(1)} %pad_maximum_fusion.14), channel_id=1, source_target_pairs={{0,8},{2,10},{4,12},{6,14},{8,0},{10,2},{12,4},{14,6},{16,24},{18,... | collective-permute-start | bytes 1769480 | tf_op jit(solution)/shard_map/ppermute | solution.py:31
  89.5 30.4 %collective-permute-start.8 = (bf16[2,2,2,48,1152]{4,3,2,1,0:T(8,128)(2,1)}, bf16[2,2,2,48,1152]{4,3,2,1,0:T(8,128)(2,1)}, u32[]{:S(2)}, u32[]{:S(2)}) collective-permute-start(bf16[2,2,2,48,1152]{4,3,2,1,0:T(8,128)(2,1)} %pad_maximum_fusion.11), channel_id=1, source_target_pairs={{0,8},{2,10},{4,12},{6,14},{8,0},{10,2},{12,4},{14,6},{16,24},{18,... | collective-permute-start | bytes 2654216 | tf_op jit(solution)/shard_map/ppermute | solution.py:31
  91.4 153.6 %collective-permute-start.16 = (bf16[2,2,2,48,1536]{4,3,2,1,0:T(8,128)(2,1)}, bf16[2,2,2,48,1536]{4,3,2,1,0:T(8,128)(2,1)}, u32[]{:S(2)}, u32[]{:S(2)}) collective-permute-start(bf16[2,2,2,48,1536]{4,3,2,1,0:T(8,128)(2,1)} %pad_maximum_fusion.7), channel_id=1, source_target_pairs={{0,2},{2,0},{4,6},{6,4},{8,10},{10,8},{12,14},{14,12},{16,18},{18,... | collective-permute-start | bytes 3538952 | tf_op jit(solution)/shard_map/ppermute | solution.py:31
  99.2 190.0 %collective-permute-start.20 = (bf16[2,2,2,48,1536]{4,3,2,0,1:T(8,128)(2,1)}, bf16[2,2,2,48,1536]{4,3,2,0,1:T(8,128)(2,1)}, u32[]{:S(2)}, u32[]{:S(2)}) collective-permute-start(bf16[2,2,2,48,1536]{4,3,2,0,1:T(8,128)(2,1)} %pad_maximum_fusion.8), channel_id=1, source_target_pairs={{0,4},{2,6},{4,0},{6,2},{8,12},{10,14},{12,8},{14,10},{16,20},{18,... | collective-permute-start | bytes 3538952 | tf_op jit(solution)/shard_map/ppermute | solution.py:31
  458.3 147.1 %collective-permute-start.46 = (bf16[2,2,2,48,1536]{4,3,2,0,1:T(8,128)(2,1)}, bf16[2,2,2,48,1536]{4,3,2,0,1:T(8,128)(2,1)}, u32[]{:S(2)}, u32[]{:S(2)}) collective-permute-start(bf16[2,2,2,48,1536]{4,3,2,0,1:T(8,128)(2,1)} %fusion.95), channel_id=1, source_target_pairs={{0,4},{2,6},{4,0},{6,2},{8,12},{10,14},{12,8},{14,10},{16,20},{18,... | collective-permute-start | bytes 3538952 | tf_op jit(solution)/shard_map/ppermute | solution.py:31
  460.1 129.7 %collective-permute-start.21 = (bf16[1024,768]{1,0:T(8,128)(2,1)}, bf16[1024,768]{1,0:T(8,128)(2,1)}, u32[]{:S(2)}, u32[]{:S(2)}) collective-permute-start(bf16[1024,768]{1,0:T(8,128)(2,1)} %fusion.68), channel_id=1, source_target_pairs={{0,1},{1,0},{2,3},{3,2},{4,5},{5,4},{6,7},{7,6},{8,9},{9,8},{10,11... | collective-permute-start | bytes 4718600 | tf_op jit(solution)/shard_map/ppermute | solution.py:31
  493.0 92.6 %collective-permute-start.23 = (bf16[1024,768]{1,0:T(8,128)(2,1)}, bf16[1024,768]{1,0:T(8,128)(2,1)}, u32[]{:S(2)}, u32[]{:S(2)}) collective-permute-start(bf16[1024,768]{1,0:T(8,128)(2,1)} %fusion.69), channel_id=1, source_target_pairs={{0,1},{1,0},{2,3},{3,2},{4,5},{5,4},{6,7},{7,6},{8,9},{9,8},{10,11... | collective-permute-start | bytes 4718600 | tf_op jit(solution)/shard_map/ppermute | solution.py:31
  529.5 56.1 %collective-permute-start.24 = (bf16[1024,768]{1,0:T(8,128)(2,1)S(1)}, bf16[1024,768]{1,0:T(8,128)(2,1)S(1)}, u32[]{:S(2)}, u32[]{:S(2)}) collective-permute-start(bf16[1024,768]{1,0:T(8,128)(2,1)S(1)} %fusion.70), channel_id=1, source_target_pairs={{0,1},{1,0},{2,3},{3,2},{4,5},{5,4},{6,7},{7,6},{8,9},{9,8},{10,11... | collective-permute-start | bytes 4718600 | tf_op jit(solution)/shard_map/ppermute | solution.py:31
  585.2 28.6 %collective-permute-start.50 = (bf16[2,2,2,48,1536]{4,3,1,2,0:T(8,128)(2,1)S(1)}, bf16[2,2,2,48,1536]{4,3,1,2,0:T(8,128)(2,1)S(1)}, u32[]{:S(2)}, u32[]{:S(2)}) collective-permute-start(bf16[2,2,2,48,1536]{4,3,1,2,0:T(8,128)(2,1)S(1)} %fusion.96), channel_id=1, source_target_pairs={{0,8},{2,10},{4,12},{6,14},{8,0},{10,2},{12,4},{14,6},{16,24},{18,... | collective-permute-start | bytes 3538952 | tf_op jit(solution)/shard_map/ppermute | solution.py:31
  609.8 13.1 %collective-permute-start.47 = (bf16[2,2,48,1536]{3,2,1,0:T(8,128)(2,1)S(1)}, bf16[2,2,48,1536]{3,2,1,0:T(8,128)(2,1)S(1)}, u32[]{:S(2)}, u32[]{:S(2)}) collective-permute-start(bf16[2,2,48,1536]{3,2,1,0:T(8,128)(2,1)S(1)} %fusion.108), channel_id=1, source_target_pairs={{0,8},{2,10},{4,12},{6,14},{8,0},{10,2},{12,4},{14,6},{16,24},{18,... | collective-permute-start | bytes 1769480 | tf_op jit(solution)/shard_map/ppermute | solution.py:31
  617.6 36.6 %collective-permute-start.51 = (bf16[2,2,48,1536]{3,2,0,1:T(8,128)(2,1)S(1)}, bf16[2,2,48,1536]{3,2,0,1:T(8,128)(2,1)S(1)}, u32[]{:S(2)}, u32[]{:S(2)}) collective-permute-start(bf16[2,2,48,1536]{3,2,0,1:T(8,128)(2,1)S(1)} %fusion.109), channel_id=1, source_target_pairs={{0,16},{2,18},{4,20},{6,22},{8,24},{10,26},{12,28},{14,30},{16,0},... | collective-permute-start | bytes 1769480 | tf_op jit(solution)/shard_map/ppermute | solution.py:31
  623.0 37.3 %collective-permute-start.48 = (bf16[2,48,1536]{2,1,0:T(8,128)(2,1)S(1)}, bf16[2,48,1536]{2,1,0:T(8,128)(2,1)S(1)}, u32[]{:S(2)}, u32[]{:S(2)}) collective-permute-start(bf16[2,48,1536]{2,1,0:T(8,128)(2,1)S(1)} %fusion.125), channel_id=1, source_target_pairs={{0,16},{2,18},{4,20},{6,22},{8,24},{10,26},{12,28},{14,30},{16,0},... | collective-permute-start | bytes 884744 | tf_op jit(solution)/shard_map/ppermute | solution.py:31
  (145 other events, 2025.7 us)
